TPU v7x, 256 devices: a whole 4x4x8 slice. The times are simulated.
256 devices in a mesh: subj: 16 (over y, x), slab: 16 (over z, core).
Axes of the slice: x: 4, y: 4, z: 8, core: 2. Of those that a mesh axis runs over, the one named last changes fastest.
Arguments:
- template: float32 [8192, 128], P('slab'), may hold values from -6 to 6
- images: float32 [16, 8192, 128], P('subj', 'slab'), may hold values from -6 to 6
- velocity: float32 [16, 3, 8192, 128], P('subj', None, 'slab'), may hold values from -6 to 6
- stiffness: float32 [8192, 128], P('slab'), may hold values from 0.1 to 1
- send_rows: int32 [16, 16, 16, 32], P('subj', 'slab'), may hold values from 0 to 511, as said below
- ref_slot: int32 [16, 8192, 8], P('subj', 'slab'), may hold values from 0 to 511, as said below
- columns: int32 [16, 8192, 8, 128], P('subj', 'slab'), may hold values from 0 to 127, as said below
- weights: bfloat16 [16, 8192, 8, 128], P('subj', 'slab'), may hold values from 0 to 0.25
Outputs:
- template_out: float32 [8192, 128], P('slab')
- velocity_out: float32 [16, 3, 8192, 128], P('subj', None, 'slab')
Inputs may be any that keep to these rules, and one draw needn't show every extreme that they name: `send_rows`: local rows of the owner slab. `ref_slot`: for each subject and each owner k and destination slab j, the referenced c lie below a count of that pair between 16 and 32; for each subject one destination slab has the count 32 from every owner. columns[s, g, b, x] differs from x by at most 2.
All inputs are finite; a program needn't handle non-finite values.
Results may differ from a plain program's by a relative error of at most 0.0003.
Values sent between devices are 32-bit elements; how exact they have to be, the bound alone decides.
A program may use at most 64 MiB of HBM per device.

v0:
```python
import jax
import jax.numpy as jnp
from jax import lax
from jax.sharding import PartitionSpec as P

YR = 256
SMOOTH = 2


force_step = 1.0
diffusion_dt = 0.16
template_rate = 2.0


def extended(cells, sides, width):
    for axis, dim in sides:
        count = lax.axis_size(axis)
        ends = count - 1
        head = lax.slice_in_dim(cells, 0, width, axis=dim)
        tail = lax.slice_in_dim(cells, cells.shape[dim] - width, cells.shape[dim], axis=dim)
        cells = jnp.concatenate(
            [
                lax.ppermute(tail, axis, [(i, (i + 1) % count) for i in range(ends)]),
                cells,
                lax.ppermute(head, axis, [((i + 1) % count, i) for i in range(ends)]),
            ],
            axis=dim,
        )
    return cells


def smooth_step(field_padded, coef_padded):
    center = field_padded[:, 1:-1]
    coef_center = coef_padded[1:-1]
    field_yx = jnp.pad(center, ((0, 0), (0, 0), (1, 1), (1, 1)))
    coef_yx = jnp.pad(coef_center, ((0, 0), (1, 1), (1, 1)))
    pairs = [
        (field_padded[:, 2:], coef_padded[2:]),
        (field_padded[:, :-2], coef_padded[:-2]),
        (field_yx[:, :, 2:, 1:-1], coef_yx[:, 2:, 1:-1]),
        (field_yx[:, :, :-2, 1:-1], coef_yx[:, :-2, 1:-1]),
        (field_yx[:, :, 1:-1, 2:], coef_yx[:, 1:-1, 2:]),
        (field_yx[:, :, 1:-1, :-2], coef_yx[:, 1:-1, :-2]),
    ]
    summed = jnp.zeros(center.shape, jnp.float32)
    for neighbour, coef_near in pairs:
        face_coef = 0.5 * (coef_center + coef_near)
        summed = summed + face_coef[None] * (neighbour - center)
    return center + diffusion_dt * summed


def read_ahead(values, offset):
    if offset > 0:
        return jnp.concatenate(
            [values[..., offset:], jnp.zeros(values.shape[:-1] + (offset,), values.dtype)], axis=-1
        )
    if offset < 0:
        return jnp.concatenate(
            [jnp.zeros(values.shape[:-1] + (-offset,), values.dtype), values[..., :offset]], axis=-1
        )
    return values


def per_device(template, images, velocity, stiffness, send_rows, ref_slot, columns, weights):
    slabs = lax.axis_size("slab")
    subjects = lax.axis_size("subj")
    capacity = send_rows.shape[3]
    rows = template.shape[0]
    width = template.shape[1]
    planes = rows // YR
    send_one = send_rows[0, 0]
    sending = template[send_one]
    received = lax.all_to_all(sending, "slab", split_axis=0, concat_axis=0, tiled=True)
    flat_rows = received.reshape(slabs * capacity, width)
    slot_one = ref_slot[0]
    offset_one = columns[0] - jnp.arange(width, dtype=jnp.int32)
    picked = flat_rows[slot_one]
    weight_f = weights[0].astype(jnp.float32)
    values = jnp.zeros(picked.shape, jnp.float32)
    for offset in range(-2, 3):
        values = values + jnp.where(offset_one == offset, read_ahead(picked, offset), 0.0)
    warped = jnp.sum(weight_f * values, axis=1)
    mismatch = warped - images[0]
    contrib = weight_f * mismatch[:, None, :]
    placed = jnp.zeros(contrib.shape, jnp.float32)
    for offset in range(-2, 3):
        placed = placed + read_ahead(jnp.where(offset_one == offset, contrib, 0.0), -offset)
    slot_grad = (
        jnp.zeros((slabs * capacity, width), jnp.float32)
        .at[slot_one.reshape(-1)]
        .add(placed.reshape(-1, width))
    )
    slot_grad = slot_grad.reshape(slabs, capacity, width)
    returned = lax.all_to_all(slot_grad, "slab", split_axis=0, concat_axis=0, tiled=True)
    row_grad = (
        jnp.zeros((rows, width), jnp.float32)
        .at[send_one.reshape(-1)]
        .add(returned.reshape(-1, width))
    )
    summed = lax.psum(row_grad, "subj")
    template_out = template - template_rate * summed / subjects
    warped_grid = warped.reshape(planes, YR, width)
    warped_padded = extended(warped_grid, (("slab", 0),), 1)
    warped_yx = jnp.pad(warped_grid, ((0, 0), (1, 1), (1, 1)))
    along_x = 0.5 * (warped_yx[:, 1:-1, 2:] - warped_yx[:, 1:-1, :-2])
    along_y = 0.5 * (warped_yx[:, 2:, 1:-1] - warped_yx[:, :-2, 1:-1])
    along_z = 0.5 * (warped_padded[2:] - warped_padded[:-2])
    slopes = jnp.stack([along_x, along_y, along_z])
    field = (
        velocity[0].reshape(3, planes, YR, width)
        - force_step * mismatch.reshape(planes, YR, width)[None] * slopes
    )
    coef_grid = stiffness.reshape(planes, YR, width)
    coef_padded = extended(coef_grid, (("slab", 0),), 1)
    for repeat in range(SMOOTH):
        field_padded = extended(field, (("slab", 1),), 1)
        field = smooth_step(field_padded, coef_padded)
    velocity_out = field.reshape(3, rows, width)[None]
    return (template_out, velocity_out)


def solution(mesh):
    return jax.shard_map(
        per_device,
        mesh=mesh,
        in_specs=(
            P("slab", None),
            P("subj", "slab", None),
            P("subj", None, "slab", None),
            P("slab", None),
            P("subj", "slab", None, None),
            P("subj", "slab", None),
            P("subj", "slab", None, None),
            P("subj", "slab", None, None),
        ),
        out_specs=(P("slab", None), P("subj", None, "slab", None)),
        check_vma=False,
    )
```

profile of v0, /device:TPU:1, one launch (start us, length us, event | category | flops | bytes accessed | tf_op | source)
XLA Modules:
  0.0 206.5 jit_solution(10799320863399200082)
XLA Ops:
  7.2 0.7 compare_select_fusion.2
  8.0 2.6 %gather_fusion = f32[512,128]{1,0:T(8,128)} fusion(f32[512,128]{1,0:T(8,128)} %param.8, s32[1024]{0:T(1024)S(1)} %pad_clamp_fusion), kind=kCustom, calls=%fused_computation | custom fusion | bytes 526336 | tf_op jit(solution)/shard_map/gather | solution.py:72
  10.6 10.0 %all-to-all-start = ((f32[16,32,128]{2,1,0:T(8,128)}), f32[16,32,128]{2,1,0:T(8,128)S(1)}, u32[]{:S(2)}, u32[]{:S(2)}) async-start(f32[16,32,128]{2,1,0:T(8,128)} %bitcast.6), calls=%async_computation | async-start | bytes 524288 | tf_op jit(solution)/shard_map/all_to_all | solution.py:73
  20.6 0.7 slice_bitcast_fusion.3
  21.3 2.0 collective-permute-start.2
  23.3 3.6 %collective-permute-start.4 = (f32[1,256,128]{2,1,0:T(8,128)}, f32[1,256,128]{2,1,0:T(8,128)}, u32[]{:S(2)}, u32[]{:S(2)}) collective-permute-start(f32[1,256,128]{2,1,0:T(8,128)} %get-tuple-element.27), channel_id=1, source_target_pairs={{0,1},{1,2},{2,3},{3,4},{4,5},{5,6},{6,7},{7,8},{8,9},{9,10},{10,1... | collective-permute-start | bytes 393224 | tf_op jit(solution)/shard_map/ppermute | solution.py:23
  27.3 0.7 reshape_squeeze.9
  28.2 4.1 %all-to-all-done = f32[16,32,128]{2,1,0:T(8,128)S(1)} async-done(((f32[16,32,128]{2,1,0:T(8,128)}), f32[16,32,128]{2,1,0:T(8,128)S(1)}, u32[]{:S(2)}, u32[]{:S(2)}) %all-to-all-start) | async-done | bytes 262176 | tf_op jit(solution)/shard_map/all_to_all | solution.py:73
  32.3 10.8 %gather_fusion.1 = f32[4096,128]{1,0:T(8,128)S(1)} fusion(f32[512,128]{1,0:T(8,128)S(1)} %bitcast.66, s32[4096]{0:T(1024)S(1)} %broadcast_clamp_fusion), kind=kCustom, calls=%fused_computation.1 | custom fusion | bytes 4210688 | tf_op jit(solution)/shard_map/gather | solution.py:77
  43.1 0.7 fusion.86
  43.8 0.7 fusion.87
  45.0 0.7 copy-done.3
  45.7 3.9 %fusion = (f32[512,128]{1,0:T(8,128)S(1)}, pred[512,8,128]{2,1,0:T(8,128)(4,1)S(1)}, pred[512,8,128]{2,1,0:T(8,128)(4,1)S(1)}, pred[512,8,128]{2,1,0:T(8,128)(4,...) fusion(f32[512,8,126]{2,1,0:T(8,128)S(1)} %get-tuple-element.13, ...), kind=kLoop, calls=%fused_computation.14 | loop fusion | flops 9371648 | bytes 16416768 | tf_op jit(solution)/shard_map/reduce_sum | solution.py:82
  49.6 0.7 slice_bitcast_fusion.1
  50.3 1.9 collective-permute-start
  52.3 3.6 %collective-permute-start.1 = (f32[1,256,128]{2,1,0:T(8,128)}, f32[1,256,128]{2,1,0:T(8,128)}, u32[]{:S(2)}, u32[]{:S(2)}) collective-permute-start(f32[1,256,128]{2,1,0:T(8,128)} %get-tuple-element.33), channel_id=1, source_target_pairs={{0,1},{1,2},{2,3},{3,4},{4,5},{5,6},{6,7},{7,8},{8,9},{9,10},{10,1... | collective-permute-start | bytes 393224 | tf_op jit(solution)/shard_map/ppermute | solution.py:23
  56.7 2.6 %slice_select_fusion.2 = (f32[512,8,127]{2,1,0:T(8,128)S(1)}, f32[512,8,127]{2,1,0:T(8,128)}) fusion(f32[512,8,128]{2,1,0:T(8,128)S(1)} %convert_multiply_fusion, pred[512,8,128]{2,1,0:T(8,128)(4,1)S(1)} %get-tuple-element.4, pred[512,8,128]{2,1,0:T(8,128)(4,1)S(1)} %get-tuple-element.6), kind=kLoop, calls=%fused_computation.17 | loop fusion | flops 1040384 | bytes 9363456 | tf_op jit(solution)/shard_map/jit(_where)/select_n | solution.py:87
  59.3 3.2 %slice_select_fusion.3 = (f32[512,8,126]{2,1,0:T(8,128)}, f32[512,8,126]{2,1,0:T(8,128)}) fusion(f32[512,8,128]{2,1,0:T(8,128)S(1)} %convert_multiply_fusion, pred[512,8,128]{2,1,0:T(8,128)(4,1)S(1)} %get-tuple-element.3, pred[512,8,128]{2,1,0:T(8,128)(4,1)S(1)} %get-tuple-element.7), kind=kLoop, calls=%fused_computation.18 | loop fusion | flops 1032192 | bytes 9289728 | tf_op jit(solution)/shard_map/jit(_where)/select_n | solution.py:87
  62.5 23.1 %scatter_custom_fusion = f32[512,128]{1,0:T(8,128)} fusion(s32[4096]{0:T(1024)S(1)} %bitcast.75, f32[512,8,126]{2,1,0:T(8,128)} %get-tuple-element.9, f32[]{:T(128)} %constant.10.clone.1, f32[512,8,127]{2,1,0:T(8,128)} %get-tuple-element.11, pred[512,8,128]{2,1,0:T(8,128)(4,1)} %get-tuple-element.5, f32[512,8,127]{2,1,0:T(8,128)S(1)} %get-tuple-element.10, ...), kind=kCustom, calls=%fused_computation.19 | custom fusion | flops 4194304 | bytes 10487296 | tf_op jit(solution)/shard_map/scatter-add | solution.py:91
  85.6 4.2 %all-to-all-start.1 = ((f32[16,32,128]{2,1,0:T(8,128)}), f32[16,32,128]{2,1,0:T(8,128)}, u32[]{:S(2)}, u32[]{:S(2)}) async-start(f32[16,32,128]{2,1,0:T(8,128)} %bitcast.71), calls=%async_computation.1 | async-start | bytes 524288 | tf_op jit(solution)/shard_map/all_to_all | solution.py:94
  89.9 1.2 fusion.90
  91.3 1.9 collective-permute-start.3
  93.2 3.8 %collective-permute-start.5 = (f32[3,1,256,128]{3,2,1,0:T(8,128)S(1)}, f32[3,1,256,128]{3,2,1,0:T(8,128)}, u32[]{:S(2)}, u32[]{:S(2)}) collective-permute-start(f32[3,1,256,128]{3,2,1,0:T(8,128)S(1)} %get-tuple-element.19), channel_id=1, source_target_pairs={{0,1},{1,2},{2,3},{3,4},{4,5},{5,6},{6,7},{7,8},{8,9},{9,10},{10,1... | collective-permute-start | bytes 1179656 | tf_op jit(solution)/shard_map/ppermute | solution.py:23
  97.1 1.2 fusion.74
  98.3 2.9 %all-to-all-done.1 = f32[16,32,128]{2,1,0:T(8,128)} async-done(((f32[16,32,128]{2,1,0:T(8,128)}), f32[16,32,128]{2,1,0:T(8,128)}, u32[]{:S(2)}, u32[]{:S(2)}) %all-to-all-start.1) | async-done | bytes 262176 | tf_op jit(solution)/shard_map/all_to_all | solution.py:94
  101.2 3.3 %scatter_custom_fusion.1 = f32[512,128]{1,0:T(8,128)} fusion(s32[512]{0:T(512)S(1)} %bitcast.76, f32[512,128]{1,0:T(8,128)} %bitcast.13, f32[]{:T(128)} %constant.10.clone.1), kind=kCustom, calls=%fused_computation.120 | custom fusion | flops 65536 | bytes 262656 | tf_op jit(solution)/shard_map/scatter-add | solution.py:98
  104.6 1.8 fusion.25
  106.5 1.9 collective-permute-start.6
  108.4 3.6 %collective-permute-start.7 = (f32[3,1,256,128]{3,2,1,0:T(8,128)S(1)}, f32[3,1,256,128]{3,2,1,0:T(8,128)}, u32[]{:S(2)}, u32[]{:S(2)}) collective-permute-start(f32[3,1,256,128]{3,2,1,0:T(8,128)S(1)} %get-tuple-element.17), channel_id=1, source_target_pairs={{0,1},{1,2},{2,3},{3,4},{4,5},{5,6},{6,7},{7,8},{8,9},{9,10},{10,1... | collective-permute-start | bytes 1179656 | tf_op jit(solution)/shard_map/ppermute | solution.py:23
  112.0 83.3 %all-reduce.14.cloned.1.call-done = f32[512,128]{1,0:T(8,128)} async-done(((f32[512,128]{1,0:T(8,128)}), f32[512,128]{1,0:T(8,128)}) %all-reduce.14.cloned.1.call-update) | async-done | bytes 262160 | tf_op jit(solution)/shard_map/psum | solution.py:100
  195.3 1.7 multiply_subtract_fusion
  197.0 2.6 %fusion.39 = f32[3,2,256,128]{3,2,1,0:T(8,128)} fusion(f32[3,2,256,128]{3,2,1,0:T(8,128)S(1)} %fusion.25, f32[3,1,256,128]{3,2,1,0:T(8,128)} %collective-permute-done.7, f32[3,1,256,128]{3,2,1,0:T(8,128)} %collective-permute-done.6, f32[2,256,128]{2,1,0:T(8,128)S(1)} %get-tuple-element.22, f32[2,256,128]{2,1,0:T(8,128)S(1)} %get-tuple-element.25, ...), kind=kLoop, calls=%fused_computation.66 | loop fusion | flops 4128768 | bytes 3932160 | tf_op jit(solution)/shard_map/add | solution.py:49
  (46 shorter events, 2.3 us)
Async XLA Ops:
  7.2 20.1 %copy-start.9 = (s32[1,1,16,32]{3,2,1,0:T(8,128)S(1)}, s32[1,1,16,32]{3,2,1,0:T(8,128)}, u32[]{:S(2)}) copy-start(s32[1,1,16,32]{3,2,1,0:T(8,128)} %param.12) | copy-start | bytes 6148
  7.2 13.4 %copy-start.5 = (f32[512,128]{1,0:T(8,128)S(1)}, f32[512,128]{1,0:T(8,128)}, u32[]{:S(2)}) copy-start(f32[512,128]{1,0:T(8,128)} %param.11) | copy-start | bytes 786436
  7.2 19.7 %copy-start.8 = (s32[1,512,8]{1,2,0:T(8,128)S(1)}, s32[1,512,8]{1,2,0:T(8,128)}, u32[]{:S(2)}) copy-start(s32[1,512,8]{1,2,0:T(8,128)} %param.13) | copy-start | bytes 49156
  10.6 21.7 %all-to-all-start = ((f32[16,32,128]{2,1,0:T(8,128)}), f32[16,32,128]{2,1,0:T(8,128)S(1)}, u32[]{:S(2)}, u32[]{:S(2)}) async-start(f32[16,32,128]{2,1,0:T(8,128)} %bitcast.6), calls=%async_computation | async-start | bytes 524288 | tf_op jit(solution)/shard_map/all_to_all | solution.py:73
  21.3 75.8 %collective-permute-start.2 = (f32[1,256,128]{2,1,0:T(8,128)}, f32[1,256,128]{2,1,0:T(8,128)}, u32[]{:S(2)}, u32[]{:S(2)}) collective-permute-start(f32[1,256,128]{2,1,0:T(8,128)} %get-tuple-element.26), channel_id=1, source_target_pairs={{1,0},{2,1},{3,2},{4,3},{5,4},{6,5},{7,6},{8,7},{9,8},{10,9},{11,1... | collective-permute-start | bytes 393224 | tf_op jit(solution)/shard_map/ppermute | solution.py:25
  23.3 73.8 %collective-permute-start.4 = (f32[1,256,128]{2,1,0:T(8,128)}, f32[1,256,128]{2,1,0:T(8,128)}, u32[]{:S(2)}, u32[]{:S(2)}) collective-permute-start(f32[1,256,128]{2,1,0:T(8,128)} %get-tuple-element.27), channel_id=1, source_target_pairs={{0,1},{1,2},{2,3},{3,4},{4,5},{5,6},{6,7},{7,8},{8,9},{9,10},{10,1... | collective-permute-start | bytes 393224 | tf_op jit(solution)/shard_map/ppermute | solution.py:23
  43.8 1.2 copy-start.1
  43.8 1.9 copy-start.3
  45.7 10.2 %copy-start.4 = (f32[1,512,128]{2,1,0:T(8,128)S(1)}, f32[1,512,128]{2,1,0:T(8,128)}, u32[]{:S(2)}) copy-start(f32[1,512,128]{2,1,0:T(8,128)} %param.9) | copy-start | bytes 786436
  50.3 39.5 %collective-permute-start = (f32[1,256,128]{2,1,0:T(8,128)}, f32[1,256,128]{2,1,0:T(8,128)S(1)}, u32[]{:S(2)}, u32[]{:S(2)}) collective-permute-start(f32[1,256,128]{2,1,0:T(8,128)} %get-tuple-element.32), channel_id=1, source_target_pairs={{1,0},{2,1},{3,2},{4,3},{5,4},{6,5},{7,6},{8,7},{9,8},{10,9},{11,1... | collective-permute-start | bytes 393224 | tf_op jit(solution)/shard_map/ppermute | solution.py:25
  52.3 37.6 %collective-permute-start.1 = (f32[1,256,128]{2,1,0:T(8,128)}, f32[1,256,128]{2,1,0:T(8,128)}, u32[]{:S(2)}, u32[]{:S(2)}) collective-permute-start(f32[1,256,128]{2,1,0:T(8,128)} %get-tuple-element.33), channel_id=1, source_target_pairs={{0,1},{1,2},{2,3},{3,4},{4,5},{5,6},{6,7},{7,8},{8,9},{9,10},{10,1... | collective-permute-start | bytes 393224 | tf_op jit(solution)/shard_map/ppermute | solution.py:23
  56.0 0.7 copy-start.2
  85.6 5.5 %copy-start.7 = (f32[1,3,512,128]{3,2,1,0:T(8,128)S(1)}, f32[1,3,512,128]{3,2,1,0:T(8,128)}, u32[]{:S(2)}) copy-start(f32[1,3,512,128]{3,2,1,0:T(8,128)} %param.10) | copy-start | bytes 2359300
  85.6 15.7 %all-to-all-start.1 = ((f32[16,32,128]{2,1,0:T(8,128)}), f32[16,32,128]{2,1,0:T(8,128)}, u32[]{:S(2)}, u32[]{:S(2)}) async-start(f32[16,32,128]{2,1,0:T(8,128)} %bitcast.71), calls=%async_computation.1 | async-start | bytes 524288 | tf_op jit(solution)/shard_map/all_to_all | solution.py:94
  89.8 105.5 %all-reduce.14.cloned.1.call-start = ((), (), s32[]{:S(2)}) async-start(), calls=%async_computation.2 | async-start | bytes 524288 | tf_op jit(solution)/shard_map/psum | solution.py:100
  91.1 6.0 %copy-start.10 = (s32[512,1]{0,1:T(1,128)S(1)}, s32[512,1]{0,1:T(1,128)}, u32[]{:S(2)}) copy-start(s32[512,1]{0,1:T(1,128)} %reshape_squeeze.9) | copy-start | bytes 6148
  91.1 6.0 %copy-start.6 = (f32[512,128]{1,0:T(8,128)S(1)}, f32[512,128]{1,0:T(8,128)}, u32[]{:S(2)}) copy-start(f32[512,128]{1,0:T(8,128)} %param.11) | copy-start | bytes 786436
  91.3 13.2 %collective-permute-start.3 = (f32[3,1,256,128]{3,2,1,0:T(8,128)S(1)}, f32[3,1,256,128]{3,2,1,0:T(8,128)}, u32[]{:S(2)}, u32[]{:S(2)}) collective-permute-start(f32[3,1,256,128]{3,2,1,0:T(8,128)S(1)} %get-tuple-element.18), channel_id=1, source_target_pairs={{1,0},{2,1},{3,2},{4,3},{5,4},{6,5},{7,6},{8,7},{9,8},{10,9},{11,1... | collective-permute-start | bytes 1179656 | tf_op jit(solution)/shard_map/ppermute | solution.py:25
  93.2 11.3 %collective-permute-start.5 = (f32[3,1,256,128]{3,2,1,0:T(8,128)S(1)}, f32[3,1,256,128]{3,2,1,0:T(8,128)}, u32[]{:S(2)}, u32[]{:S(2)}) collective-permute-start(f32[3,1,256,128]{3,2,1,0:T(8,128)S(1)} %get-tuple-element.19), channel_id=1, source_target_pairs={{0,1},{1,2},{2,3},{3,4},{4,5},{5,6},{6,7},{7,8},{8,9},{9,10},{10,1... | collective-permute-start | bytes 1179656 | tf_op jit(solution)/shard_map/ppermute | solution.py:23
  104.6 90.8 %copy-start = (f32[512,128]{1,0:T(8,128)S(1)}, f32[512,128]{1,0:T(8,128)}, u32[]{:S(2)}) copy-start(f32[512,128]{1,0:T(8,128)} %param.8) | copy-start | bytes 786436
  106.5 90.6 %collective-permute-start.6 = (f32[3,1,256,128]{3,2,1,0:T(8,128)S(1)}, f32[3,1,256,128]{3,2,1,0:T(8,128)}, u32[]{:S(2)}, u32[]{:S(2)}) collective-permute-start(f32[3,1,256,128]{3,2,1,0:T(8,128)S(1)} %get-tuple-element.16), channel_id=1, source_target_pairs={{1,0},{2,1},{3,2},{4,3},{5,4},{6,5},{7,6},{8,7},{9,8},{10,9},{11,1... | collective-permute-start | bytes 1179656 | tf_op jit(solution)/shard_map/ppermute | solution.py:25
  108.4 88.6 %collective-permute-start.7 = (f32[3,1,256,128]{3,2,1,0:T(8,128)S(1)}, f32[3,1,256,128]{3,2,1,0:T(8,128)}, u32[]{:S(2)}, u32[]{:S(2)}) collective-permute-start(f32[3,1,256,128]{3,2,1,0:T(8,128)S(1)} %get-tuple-element.17), channel_id=1, source_target_pairs={{0,1},{1,2},{2,3},{3,4},{4,5},{5,6},{6,7},{7,8},{8,9},{9,10},{10,1... | collective-permute-start | bytes 1179656 | tf_op jit(solution)/shard_map/ppermute | solution.py:23
Sparse Core Ops, SparseCore 0:
  104.7 90.6 all-reduce.13
where the time goes:
time: 207 us
  waiting for transfers between devices  90.3 us (44%)
  other arithmetic  45.8 us (22%)
  starting transfers between devices  36.7 us (18%)
  local copies, waits for them, and re-layouts  19.3 us (9%)
  between operations  14.4 us (7%)
    psum x1, waiting for transfers between devices, per_device(): summed = lax.psum(row_grad, 'subj')  83.3 us
    scatter-add x1, other arithmetic, per_device(): slot_grad = jnp.zeros((slabs * capacity, width), jnp.float32).at[slot_one...  23.1 us
    ppermute x4, starting transfers between devices, extended(): lax.ppermute(tail, axis, [(i, (i + 1) % count) for i in range(ends)])  14.7 us
    gather x1, local copies, waits for them, and re-layouts, per_device(): picked = flat_rows[slot_one]  10.8 us
    all_to_all x1, starting transfers between devices, per_device(): lax.all_to_all(sending, 'slab', split_axis=0, concat_axis=0, tiled=True)  9.98 us
    ppermute x4, starting transfers between devices, extended(): lax.ppermute(head, axis, [((i + 1) % count, i) for i in range(ends)])  7.75 us
    select_n x2, other arithmetic, per_device(): jnp.where(offset_one == offset, contrib, 0.0)  5.79 us
    add x2, other arithmetic, smooth_step(): return center + diffusion_dt * summed  4.45 us
  transfers between devices with their start and end apart: 11, of which 3 were waited for; matrix products, arithmetic and copies ran while one was open for 28% of the time, Pallas kernels for 0%

commit v1 on v0

v1 whole, which is shorter than its diff:
```python
import functools

import jax
import jax.numpy as jnp
from jax import lax
from jax.experimental import pallas as pl
from jax.experimental.pallas import tpu as pltpu
from jax.sharding import PartitionSpec as P

YR = 256
NB = 8
HALF_DT = 0.5 * 0.16
FORCE = 1.0
RATE = 2.0
OFFSETS = (-2, -1, 0, 1, 2)
BF = jnp.bfloat16
F32 = jnp.float32


def halves(x):
    hi = x.astype(BF)
    lo = (x - hi.astype(F32)).astype(BF)
    return hi, lo


def far_first(n):
    return sorted(range(1, n), key=lambda d: -min(d, n - d))


def kernel(
    subjects, slabs, cap,
    tmpl, img, vel, stiff, send, slot_t, cols, wts,
    tout, vout,
    tmpl_v, img_v, vel_v, send_v, slot_v, cols_v, wts_v, w32, colb, wb, wd, oh, oht, os, ost,
    outbox, inbox, t2, warp, mis, place, grad, retbox, rowg, subbox, tnew, coef, stif, field, field1, field2,
    load_sem, a_send, a_recv, b_send, b_recv, c_send, c_recv, d_send, d_recv, h_send, h_recv,
):
    rows, width = tmpl_v.shape
    slots = slabs * cap
    part = rows // subjects
    me_s = lax.axis_index("subj")
    me_k = lax.axis_index("slab")

    pairs = (
        (send, send_v), (tmpl, tmpl_v), (slot_t, slot_v), (cols, cols_v), (wts, wts_v),
        (stiff, stif.at[pl.ds(2 * YR, rows), :]), (img, img_v), (vel, vel_v),
    )
    loads = [pltpu.make_async_copy(a, b, load_sem.at[i]) for i, (a, b) in enumerate(pairs)]
    for load in loads:
        load.start()

    barrier = pltpu.get_barrier_semaphore()
    for d in range(1, slabs):
        pl.semaphore_signal(barrier, inc=1, device_id={"slab": lax.rem(me_k + d, slabs)})
    for d in range(1, subjects):
        pl.semaphore_signal(barrier, inc=1, device_id={"subj": lax.rem(me_s + d, subjects)})

    def peers(axis, n, me, src, dst, send_sem, recv_sem):
        out = []
        for d in far_first(n):
            to = lax.rem(me + d, n)
            come = lax.rem(me + n - d, n)
            go = pltpu.make_async_remote_copy(
                src_ref=src(to), dst_ref=dst(me), send_sem=send_sem.at[to], recv_sem=recv_sem.at[me],
                device_id={axis: to},
            )
            got = pltpu.make_async_remote_copy(
                src_ref=src(to), dst_ref=dst(come), send_sem=send_sem.at[to], recv_sem=recv_sem.at[come],
                device_id={axis: to},
            )
            out.append((go, got))
        return out

    loads[0].wait()
    send_c = jnp.transpose(send_v[0, 0])
    lane_r = lax.broadcasted_iota(jnp.int32, (cap, rows), 1)
    for j in range(slabs):
        os[pl.ds(j * cap, cap), :] = jnp.where(send_c[:, j : j + 1] == lane_r, 1.0, 0.0).astype(BF)
    loads[1].wait()
    hi, lo = halves(tmpl_v[...])
    both = jnp.dot(os[...], jnp.concatenate([hi, lo], axis=1), preferred_element_type=F32)
    outbox[...] = both[:, :width] + both[:, width:]

    pl.semaphore_wait(barrier, slabs - 1 + subjects - 1)
    first = peers(
        "slab", slabs, me_k,
        lambda j: outbox.at[pl.ds(j * cap, cap), :], lambda k: inbox.at[pl.ds(k * cap, cap), :], a_send, a_recv,
    )
    for go, _ in first:
        go.start()
    own = pl.ds(pl.multiple_of(me_k * cap, cap), cap)
    inbox[own, :] = outbox[own, :]

    loads[2].wait()
    slot_c = jnp.transpose(slot_v[0])
    lane_q = lax.broadcasted_iota(jnp.int32, (rows, slots), 1)
    sub_q = lax.broadcasted_iota(jnp.int32, (slots, rows), 0)
    for b in range(NB):
        oh[b] = jnp.where(slot_c[:, b : b + 1] == lane_q, 1.0, 0.0).astype(BF)
        oht[b] = jnp.where(sub_q == slot_v[0, b : b + 1, :], 1.0, 0.0).astype(BF)
    ost[...] = jnp.transpose(os[...].astype(F32)).astype(BF)
    loads[3].wait()
    loads[4].wait()
    w32[...] = wts_v[...].astype(F32)
    lane = lax.broadcasted_iota(jnp.int32, (rows, width), 1)
    for b in range(NB):
        col = cols_v[pl.ds(b, rows, stride=NB), :]
        wgt = w32[pl.ds(b, rows, stride=NB), :]
        colb[b] = col
        wb[b] = wgt
        off = col - lane
        for n, d in enumerate(OFFSETS):
            kept = jnp.where(off == d, wgt, 0.0)
            wd[b, n] = pltpu.roll(kept, d % width, 1) if d else kept

    for _, got in first:
        got.wait_recv()
    hi, lo = halves(inbox[...])
    t2[:, :width] = hi
    t2[:, width:] = lo
    warp[pl.ds(YR, rows), :] = jnp.zeros((rows, width), F32)

    @pl.loop(0, NB)
    def _(b):
        both = jnp.dot(oh[b], t2[...], preferred_element_type=F32)
        picked = both[:, :width] + both[:, width:]
        values = jnp.take_along_axis(picked, colb[b], axis=1, mode="promise_in_bounds")
        warp[pl.ds(YR, rows), :] += wb[b] * values

    low = lax.rem(me_k + slabs - 1, slabs)
    high = lax.rem(me_k + 1, slabs)

    def halo(ref, lead, depth, i):
        inner = rows
        at = lambda start: ref.at[lead + (pl.ds(start, depth), slice(None))]
        base = depth
        down = pltpu.make_async_remote_copy(
            src_ref=at(base), dst_ref=at(base + inner), send_sem=h_send.at[i], recv_sem=h_recv.at[i],
            device_id={"slab": low},
        )
        up = pltpu.make_async_remote_copy(
            src_ref=at(base + inner - depth), dst_ref=at(0), send_sem=h_send.at[i + 1], recv_sem=h_recv.at[i + 1],
            device_id={"slab": high},
        )
        return down, up

    def halo_start(h):
        pl.when(me_k > 0)(h[0].start)
        pl.when(me_k < slabs - 1)(h[1].start)

    def halo_got(h):
        pl.when(me_k < slabs - 1)(h[0].wait_recv)
        pl.when(me_k > 0)(h[1].wait_recv)

    def halo_sent(h):
        pl.when(me_k > 0)(h[0].wait_send)
        pl.when(me_k < slabs - 1)(h[1].wait_send)

    @pl.when(me_k == 0)
    def _():
        warp[pl.ds(0, YR), :] = jnp.zeros((YR, width), F32)
        stif[pl.ds(0, 2 * YR), :] = jnp.zeros((2 * YR, width), F32)
        field[:, pl.ds(0, 2 * YR), :] = jnp.zeros((3, 2 * YR, width), F32)

    @pl.when(me_k == slabs - 1)
    def _():
        warp[pl.ds(YR + rows, YR), :] = jnp.zeros((YR, width), F32)
        stif[pl.ds(2 * YR + rows, 2 * YR), :] = jnp.zeros((2 * YR, width), F32)
        field[:, pl.ds(2 * YR + rows, 2 * YR), :] = jnp.zeros((3, 2 * YR, width), F32)

    warp_halo = halo(warp, (), YR, 0)
    stif_halo = halo(stif, (), 2 * YR, 2)
    field_halo = [halo(field, (a,), 2 * YR, 4 + 2 * a) for a in range(3)]
    halo_start(warp_halo)
    loads[5].wait()
    halo_start(stif_halo)

    loads[6].wait()
    mis[2] = warp[pl.ds(YR, rows), :] - img_v[0]
    for n, d in enumerate(OFFSETS):
        if d:
            mis[n] = pltpu.roll(mis[2], d % width, 1)
    grad[...] = jnp.zeros((slots, 2 * width), F32)

    @pl.loop(0, NB)
    def _(b):
        total = wd[b, 0] * mis[0]
        for n in range(1, len(OFFSETS)):
            total = total + wd[b, n] * mis[n]
        hi, lo = halves(total)
        place[:, :width] = hi
        place[:, width:] = lo
        grad[...] += jnp.dot(oht[b], place[...], preferred_element_type=F32)

    for go, _ in first:
        go.wait_send()
    outbox[...] = grad[:, :width] + grad[:, width:]
    second = peers(
        "slab", slabs, me_k,
        lambda j: outbox.at[pl.ds(j * cap, cap), :], lambda k: retbox.at[pl.ds(k * cap, cap), :], b_send, b_recv,
    )
    for go, _ in second:
        go.start()
    retbox[own, :] = outbox[own, :]

    halo_got(warp_halo)
    loads[7].wait()
    lane_p = lax.broadcasted_iota(jnp.int32, (YR, width), 1)
    row_p = lax.broadcasted_iota(jnp.int32, (YR, width), 0)

    def shifted(x):
        left = jnp.where(lane_p == 0, 0.0, pltpu.roll(x, 1, 1))
        right = jnp.where(lane_p == width - 1, 0.0, pltpu.roll(x, width - 1, 1))
        above = jnp.where(row_p == 0, 0.0, pltpu.roll(x, 1, 0))
        below = jnp.where(row_p == YR - 1, 0.0, pltpu.roll(x, YR - 1, 0))
        return left, right, above, below

    @pl.loop(0, rows // YR)
    def _(p):
        here = pl.ds(pl.multiple_of(p * YR, YR), YR)
        left, right, above, below = shifted(warp[pl.ds(pl.multiple_of((p + 1) * YR, YR), YR), :])
        before = warp[here, :]
        after = warp[pl.ds(pl.multiple_of((p + 2) * YR, YR), YR), :]
        force = (0.5 * FORCE) * mis[2, here, :]
        there = pl.ds(pl.multiple_of((p + 2) * YR, YR), YR)
        field[0, there, :] = vel_v[0, 0, here, :] - force * (right - left)
        field[1, there, :] = vel_v[0, 1, here, :] - force * (below - above)
        field[2, there, :] = vel_v[0, 2, here, :] - force * (after - before)

    for h in field_halo:
        halo_start(h)

    halo_got(stif_halo)

    @pl.loop(0, rows // YR + 2)
    def _(p):
        plane = me_k * (rows // YR) + p
        inside = jnp.where(jnp.logical_and(plane >= 1, plane <= slabs * (rows // YR)), 1.0, 0.0)
        here = pl.ds(pl.multiple_of(p * YR, YR), YR)
        centre = stif[pl.ds(pl.multiple_of((p + 1) * YR, YR), YR), :]
        before = stif[here, :]
        after = stif[pl.ds(pl.multiple_of((p + 2) * YR, YR), YR), :]
        near = shifted(centre)
        scale = inside * HALF_DT
        edges = (lane_p == 0, lane_p == width - 1, row_p == 0, row_p == YR - 1)
        spent = 6.0 * centre + before + after
        for n in range(4):
            coef[n, here, :] = jnp.where(edges[n], 0.0, scale * (centre + near[n]))
            spent = spent + near[n]
        coef[4, here, :] = scale * (centre + before)
        coef[5, here, :] = scale * (centre + after)
        coef[6, here, :] = inside - scale * spent

    for _, got in second:
        got.wait_recv()
    hi, lo = halves(retbox[...])
    both = jnp.dot(ost[...], jnp.concatenate([hi, lo], axis=1), preferred_element_type=F32)
    rowg[...] = both[:, :width] + both[:, width:]
    third = peers(
        "subj", subjects, me_s,
        lambda s: rowg.at[pl.ds(s * part, part), :], lambda s: subbox.at[pl.ds(s * part, part), :], c_send, c_recv,
    )
    for go, _ in third:
        go.start()
    mine = pl.ds(pl.multiple_of(me_s * part, part), part)
    subbox[mine, :] = rowg[mine, :]

    for _, got in third:
        got.wait_recv()
    total = subbox[pl.ds(0, part), :]
    for s in range(1, subjects):
        total = total + subbox[pl.ds(s * part, part), :]
    tnew[mine, :] = tmpl_v[mine, :] - (RATE / subjects) * total
    fourth = peers(
        "subj", subjects, me_s,
        lambda s: tnew.at[mine, :], lambda s: tnew.at[pl.ds(pl.multiple_of(s * part, part), part), :], d_send, d_recv,
    )
    for go, _ in fourth:
        go.start()

    def step(src, lead, p, q):
        at = lambda i: pl.ds(pl.multiple_of(i * YR, YR), YR)
        x = src[lead, at(p), :]
        c = lambda n: coef[n, at(q), :]
        out = c(6) * x
        out = out + c(0) * pltpu.roll(x, 1, 1)
        out = out + c(1) * pltpu.roll(x, width - 1, 1)
        out = out + c(2) * pltpu.roll(x, 1, 0)
        out = out + c(3) * pltpu.roll(x, YR - 1, 0)
        out = out + c(4) * src[lead, at(p - 1), :]
        return out + c(5) * src[lead, at(p + 1), :]

    stores = []
    for a in range(3):
        halo_got(field_halo[a])

        @pl.loop(0, rows // YR + 2)
        def _(p):
            field1[a, pl.ds(pl.multiple_of(p * YR, YR), YR), :] = step(field, a, p + 1, p)

        @pl.loop(0, rows // YR)
        def _(p):
            field2[a, pl.ds(pl.multiple_of(p * YR, YR), YR), :] = step(field1, a, p + 1, p + 1)

        stores.append(pltpu.make_async_copy(field2.at[a], vout.at[0, a], load_sem.at[a]))
        stores[-1].start()

    for _, got in fourth:
        got.wait_recv()
    stores.append(pltpu.make_async_copy(tnew, tout, load_sem.at[3]))
    stores[-1].start()
    for group in (second, third, fourth):
        for go, _ in group:
            go.wait_send()
    for h in (warp_halo, stif_halo, *field_halo):
        halo_sent(h)
    for store in stores:
        store.wait()


def per_device(subjects, slabs, template, images, velocity, stiffness, send_rows, ref_slot, columns, weights):
    rows, width = template.shape
    cap = send_rows.shape[3]
    slots = slabs * cap
    planes = rows // YR
    any_space = pl.BlockSpec(memory_space=pl.ANY)
    dma = pltpu.SemaphoreType.DMA
    vm = pltpu.VMEM
    scratch = [
        vm((rows, width), F32),
        vm((1, rows, width), F32),
        vm((1, 3, rows, width), F32),
        vm((1, 1, slabs, cap), jnp.int32),
        vm((1, NB, rows), jnp.int32),
        vm((rows * NB, width), jnp.int32),
        vm((rows * NB, width), BF),
        vm((rows * NB, width), F32),
        vm((NB, rows, width), jnp.int32),
        vm((NB, rows, width), F32),
        vm((NB, len(OFFSETS), rows, width), F32),
        vm((NB, rows, slots), BF),
        vm((NB, slots, rows), BF),
        vm((slots, rows), BF),
        vm((rows, slots), BF),
        vm((slots, width), F32),
        vm((slots, width), F32),
        vm((slots, 2 * width), BF),
        vm((rows + 2 * YR, width), F32),
        vm((len(OFFSETS), rows, width), F32),
        vm((rows, 2 * width), BF),
        vm((slots, 2 * width), F32),
        vm((slots, width), F32),
        vm((rows, width), F32),
        vm((rows, width), F32),
        vm((rows, width), F32),
        vm((7, rows + 2 * YR, width), F32),
        vm((rows + 4 * YR, width), F32),
        vm((3, rows + 4 * YR, width), F32),
        vm((3, rows + 2 * YR, width), F32),
        vm((3, rows, width), F32),
        dma((8,)),
        dma((slabs,)), dma((slabs,)), dma((slabs,)), dma((slabs,)),
        dma((subjects,)), dma((subjects,)), dma((subjects,)), dma((subjects,)),
        dma((10,)), dma((10,)),
    ]
    return pl.pallas_call(
        functools.partial(kernel, subjects, slabs, cap),
        out_shape=(
            jax.ShapeDtypeStruct((rows, width), F32),
            jax.ShapeDtypeStruct((1, 3, rows, width), F32),
        ),
        in_specs=[any_space] * 8,
        out_specs=(any_space, any_space),
        scratch_shapes=scratch,
        compiler_params=pltpu.CompilerParams(
            collective_id=0, has_side_effects=True, vmem_limit_bytes=56 * 2**20
        ),
    )(
        template, images, velocity, stiffness, send_rows,
        jnp.transpose(ref_slot, (0, 2, 1)),
        columns.reshape(rows * NB, width),
        weights.reshape(rows * NB, width),
    )


def solution(mesh):
    return jax.shard_map(
        functools.partial(per_device, mesh.shape["subj"], mesh.shape["slab"]),
        mesh=mesh,
        in_specs=(
            P("slab", None),
            P("subj", "slab", None),
            P("subj", None, "slab", None),
            P("slab", None),
            P("subj", "slab", None, None),
            P("subj", "slab", None),
            P("subj", "slab", None, None),
            P("subj", "slab", None, None),
        ),
        out_specs=(P("slab", None), P("subj", None, "slab", None)),
        check_vma=False,
    )
```

time: 207 us -> 52.2 us (0.25)
  waiting for transfers between devices: 90.3 us -> 0 us
  Pallas kernels: 0 us -> 47.7 us
  other arithmetic: 45.8 us -> 0 us
  starting transfers between devices: 36.7 us -> 0 us
  local copies, waits for them, and re-layouts: 19.3 us -> 3.73 us
  between operations: 14.4 us -> 0.64 us
    psum x1 -> x0, waiting for transfers between devices: 83.3 us -> none  [per_device(): summed = lax.psum(row_grad, 'subj')]
    pallas_call x0 -> x1, Pallas kernels: none -> 47.7 us  [per_device(): pl.pallas_call(functools.partial(kernel, subjects, slabs, cap), out_shape...]
    scatter-add x2 -> x0, other arithmetic: 26.4 us -> none  [the longest x1 23.1 us: per_device(): slot_grad = jnp.zeros((slabs * capacity, width), jnp.float32).at[slot_one...]
    ppermute x8 -> x0, starting transfers between devices: 22.4 us -> none  [the longest x4 14.7 us: extended(): lax.ppermute(tail, axis, [(i, (i + 1) % count) for i in range(ends)])]
    all_to_all x2 -> x0, starting transfers between devices: 14.2 us -> none  [the longest x1 9.98 us: per_device(): lax.all_to_all(sending, 'slab', split_axis=0, concat_axis=0, tiled=True)]
    gather x2 -> x0, local copies, waits for them, and re-layouts: 13.4 us -> none  [the longest x1 10.8 us: per_device(): picked = flat_rows[slot_one]]
    all_to_all x2 -> x0, waiting for transfers between devices: 6.98 us -> none  [the longest x1 4.08 us: per_device(): lax.all_to_all(sending, 'slab', split_axis=0, concat_axis=0, tiled=True)]
    select_n x6 -> x0, other arithmetic: 6.56 us -> none  [the longest x2 5.79 us: per_device(): jnp.where(offset_one == offset, contrib, 0.0)]
  transfers between devices with their start and end apart: 11 -> 0, of which waited for: 3 -> 0; matrix products, arithmetic and copies ran while one was open for 28% -> 0% of each run, Pallas kernels for 0% -> 0%
where the time goes in v1:
time: 52.2 us; the launch traced here: 52.1 us
  Pallas kernels  47.7 us (91%)
  local copies, waits for them, and re-layouts  3.73 us (7%)
  between operations  0.64 us (1%)
    pallas_call x1, Pallas kernels, per_device(): pl.pallas_call(functools.partial(kernel, subjects, slabs, cap), out_shape...  47.7 us
    unnamed x2, local copies, waits for them, and re-layouts  3.73 us

profile of v1, /device:TPU:1, one launch (start us, length us, event | category | flops | bytes accessed | tf_op | source)
XLA Modules:
  0.0 52.1 jit_solution(16696405177022065042)
XLA Ops:
  0.6 47.7 %shard_map.95 = (f32[512,128]{1,0:T(8,128)}, f32[1,3,512,128]{3,2,1,0:T(8,128)}) custom-call(f32[512,128]{1,0:T(8,128)} %tmpl.1, f32[1,512,128]{2,1,0:T(8,128)} %img.1, f32[1,3,512,128]{3,2,1,0:T(8,128)} %vel.1, f32[512,128]{1,0:T(8,128)} %stiff.1, s32[1,1,16,32]{3,2,1,0:T(8,128)} %send.1, s32[1,8,512]{2,1,0:T(8,128)} %bitcast.5, s32[4096,128]{1,0:T(8,128)} %bitcast.3, ...), custom_call_target="tpu_custom_call" | custom-call | tf_op jit(solution)/shard_map/pallas_call | solution.py:366
  48.3 1.7 %copy.12 = f32[512,128]{1,0:T(8,128)} copy(f32[512,128]{1,0:T(8,128)} %get-tuple-element.4) | data formatting | bytes 524288
  50.0 2.1 %copy.13 = f32[1,3,512,128]{3,2,1,0:T(8,128)} copy(f32[1,3,512,128]{3,2,1,0:T(8,128)} %get-tuple-element.5) | data formatting | bytes 1572864

commit v2 on v1

--- a/solution.py
+++ b/solution.py
@@ -32,8 +32,8 @@
     tmpl, img, vel, stiff, send, slot_t, cols, wts,
     tout, vout,
     tmpl_v, img_v, vel_v, send_v, slot_v, cols_v, wts_v, w32, colb, wb, wd, oh, oht, os, ost,
-    outbox, inbox, t2, warp, mis, place, grad, retbox, rowg, subbox, tnew, coef, stif, field, field1, field2,
-    load_sem, a_send, a_recv, b_send, b_recv, c_send, c_recv, d_send, d_recv, h_send, h_recv,
+    outbox, inbox, t2, warp, mis, place, retbox, rowg, subbox, coef, stif, field, field1,
+    load_sem, a_send, a_recv, b_send, b_recv, c_send, c_recv, d_send, d_recv, e_send, e_recv, h_send, h_recv,
 ):
     rows, width = tmpl_v.shape
     slots = slabs * cap
@@ -81,7 +81,30 @@
     both = jnp.dot(os[...], jnp.concatenate([hi, lo], axis=1), preferred_element_type=F32)
     outbox[...] = both[:, :width] + both[:, width:]
 
+    odd = lax.rem(me_k, 2)
+    other = me_k + 1 - 2 * odd
+    across = me_k - 1 + 2 * odd
+    linked = jnp.logical_and(across >= 0, across < slabs)
+    mine = pl.ds(pl.multiple_of(me_s * part, part), part)
+    low_at, own_at, high_at = 0, 2 * YR, 2 * YR + rows
+    far_in = low_at + odd * (high_at - low_at)
+    far_out = high_at - odd * (high_at - low_at)
+    stif_near = pltpu.make_async_remote_copy(
+        src_ref=stif.at[pl.ds(own_at, rows), :], dst_ref=stif.at[pl.ds(pl.multiple_of(far_in, rows), rows), :],
+        send_sem=h_send.at[2], recv_sem=h_recv.at[2], device_id={"slab": other},
+    )
+
+    def stif_rows(start):
+        return stif.at[pl.ds(pl.multiple_of(start, part), part), :]
+
+    stif_far = pltpu.make_async_remote_copy(
+        src_ref=stif_rows(own_at + me_s * part), dst_ref=stif_rows(far_out + me_s * part),
+        send_sem=h_send.at[3], recv_sem=h_recv.at[3], device_id={"slab": jnp.clip(across, 0, slabs - 1)},
+    )
+    loads[5].wait()
+
     pl.semaphore_wait(barrier, slabs - 1 + subjects - 1)
+    pl.when(linked)(stif_far.start)
     first = peers(
         "slab", slabs, me_k,
         lambda j: outbox.at[pl.ds(j * cap, cap), :], lambda k: inbox.at[pl.ds(k * cap, cap), :], a_send, a_recv,
@@ -90,6 +113,8 @@
         go.start()
     own = pl.ds(pl.multiple_of(me_k * cap, cap), cap)
     inbox[own, :] = outbox[own, :]
+
+    stif_near.start()
 
     loads[2].wait()
     slot_c = jnp.transpose(slot_v[0])
@@ -97,7 +122,7 @@
     sub_q = lax.broadcasted_iota(jnp.int32, (slots, rows), 0)
     for b in range(NB):
         oh[b] = jnp.where(slot_c[:, b : b + 1] == lane_q, 1.0, 0.0).astype(BF)
-        oht[b] = jnp.where(sub_q == slot_v[0, b : b + 1, :], 1.0, 0.0).astype(BF)
+        oht[:, pl.ds(b * rows, rows)] = jnp.where(sub_q == slot_v[0, b : b + 1, :], 1.0, 0.0).astype(BF)
     ost[...] = jnp.transpose(os[...].astype(F32)).astype(BF)
     loads[3].wait()
     loads[4].wait()
@@ -113,19 +138,33 @@
             kept = jnp.where(off == d, wgt, 0.0)
             wd[b, n] = pltpu.roll(kept, d % width, 1) if d else kept
 
+    shared = peers(
+        "subj", subjects, me_s,
+        lambda s: stif_rows(far_in + me_s * part), lambda s: stif_rows(far_in + s * part), e_send, e_recv,
+    )
+
+    @pl.when(linked)
+    def _():
+        stif_far.wait_recv()
+        for go, _ in shared:
+            go.start()
+
     for _, got in first:
         got.wait_recv()
     hi, lo = halves(inbox[...])
     t2[:, :width] = hi
     t2[:, width:] = lo
-    warp[pl.ds(YR, rows), :] = jnp.zeros((rows, width), F32)
-
-    @pl.loop(0, NB)
-    def _(b):
-        both = jnp.dot(oh[b], t2[...], preferred_element_type=F32)
-        picked = both[:, :width] + both[:, width:]
-        values = jnp.take_along_axis(picked, colb[b], axis=1, mode="promise_in_bounds")
-        warp[pl.ds(YR, rows), :] += wb[b] * values
+    block = rows // 2
+    for c in range(2):
+        here = pl.ds(c * block, block)
+        total = None
+        for b in range(NB):
+            both = jnp.dot(oh[b, here, :], t2[...], preferred_element_type=F32)
+            picked = both[:, :width] + both[:, width:]
+            values = jnp.take_along_axis(picked, colb[b, here, :], axis=1, mode="promise_in_bounds")
+            term = wb[b, here, :] * values
+            total = term if total is None else total + term
+        warp[pl.ds(YR + c * block, block), :] = total
 
     low = lax.rem(me_k + slabs - 1, slabs)
     high = lax.rem(me_k + 1, slabs)
@@ -169,32 +208,29 @@
         field[:, pl.ds(2 * YR + rows, 2 * YR), :] = jnp.zeros((3, 2 * YR, width), F32)
 
     warp_halo = halo(warp, (), YR, 0)
-    stif_halo = halo(stif, (), 2 * YR, 2)
     field_halo = [halo(field, (a,), 2 * YR, 4 + 2 * a) for a in range(3)]
     halo_start(warp_halo)
-    loads[5].wait()
-    halo_start(stif_halo)
 
     loads[6].wait()
     mis[2] = warp[pl.ds(YR, rows), :] - img_v[0]
     for n, d in enumerate(OFFSETS):
         if d:
             mis[n] = pltpu.roll(mis[2], d % width, 1)
-    grad[...] = jnp.zeros((slots, 2 * width), F32)
-
-    @pl.loop(0, NB)
-    def _(b):
-        total = wd[b, 0] * mis[0]
-        for n in range(1, len(OFFSETS)):
-            total = total + wd[b, n] * mis[n]
-        hi, lo = halves(total)
-        place[:, :width] = hi
-        place[:, width:] = lo
-        grad[...] += jnp.dot(oht[b], place[...], preferred_element_type=F32)
+    block = rows // 8
+    for b in range(NB):
+        for c in range(8):
+            here = pl.ds(c * block, block)
+            total = wd[b, 0, here, :] * mis[0, here, :]
+            for n in range(1, len(OFFSETS)):
+                total = total + wd[b, n, here, :] * mis[n, here, :]
+            hi, lo = halves(total)
+            place[pl.ds(b * rows + c * block, block), :width] = hi
+            place[pl.ds(b * rows + c * block, block), width:] = lo
+    both = jnp.dot(oht[...], place[...], preferred_element_type=F32)
 
     for go, _ in first:
         go.wait_send()
-    outbox[...] = grad[:, :width] + grad[:, width:]
+    outbox[...] = both[:, :width] + both[:, width:]
     second = peers(
         "slab", slabs, me_k,
         lambda j: outbox.at[pl.ds(j * cap, cap), :], lambda k: retbox.at[pl.ds(k * cap, cap), :], b_send, b_recv,
@@ -230,7 +266,12 @@
     for h in field_halo:
         halo_start(h)
 
-    halo_got(stif_halo)
+    stif_near.wait_recv()
+
+    @pl.when(linked)
+    def _():
+        for _, got in shared:
+            got.wait_recv()
 
     @pl.loop(0, rows // YR + 2)
     def _(p):
@@ -262,7 +303,6 @@
     )
     for go, _ in third:
         go.start()
-    mine = pl.ds(pl.multiple_of(me_s * part, part), part)
     subbox[mine, :] = rowg[mine, :]
 
     for _, got in third:
@@ -270,10 +310,10 @@
     total = subbox[pl.ds(0, part), :]
     for s in range(1, subjects):
         total = total + subbox[pl.ds(s * part, part), :]
-    tnew[mine, :] = tmpl_v[mine, :] - (RATE / subjects) * total
+    tout[mine, :] = tmpl_v[mine, :] - (RATE / subjects) * total
     fourth = peers(
         "subj", subjects, me_s,
-        lambda s: tnew.at[mine, :], lambda s: tnew.at[pl.ds(pl.multiple_of(s * part, part), part), :], d_send, d_recv,
+        lambda s: tout.at[mine, :], lambda s: tout.at[pl.ds(pl.multiple_of(s * part, part), part), :], d_send, d_recv,
     )
     for go, _ in fourth:
         go.start()
@@ -290,8 +330,7 @@
         out = out + c(4) * src[lead, at(p - 1), :]
         return out + c(5) * src[lead, at(p + 1), :]
 
-    stores = []
-    for a in range(3):
+    def diffuse(a):
         halo_got(field_halo[a])
 
         @pl.loop(0, rows // YR + 2)
@@ -300,22 +339,34 @@
 
         @pl.loop(0, rows // YR)
         def _(p):
-            field2[a, pl.ds(pl.multiple_of(p * YR, YR), YR), :] = step(field1, a, p + 1, p + 1)
-
-        stores.append(pltpu.make_async_copy(field2.at[a], vout.at[0, a], load_sem.at[a]))
-        stores[-1].start()
+            vout[0, a, pl.ds(pl.multiple_of(p * YR, YR), YR), :] = step(field1, a, p + 1, p + 1)
+
+    for a in range(3):
+        diffuse(a)
 
     for _, got in fourth:
         got.wait_recv()
-    stores.append(pltpu.make_async_copy(tnew, tout, load_sem.at[3]))
-    stores[-1].start()
     for group in (second, third, fourth):
         for go, _ in group:
             go.wait_send()
-    for h in (warp_halo, stif_halo, *field_halo):
+    for h in (warp_halo, *field_halo):
         halo_sent(h)
-    for store in stores:
-        store.wait()
+    stif_near.wait_send()
+
+    @pl.when(linked)
+    def _():
+        stif_far.wait_send()
+        for go, _ in shared:
+            go.wait_send()
+
+
+def store(template, velocity, tout, vout, sem):
+    one = pltpu.make_async_copy(velocity, vout, sem.at[0])
+    two = pltpu.make_async_copy(template, tout, sem.at[1])
+    one.start()
+    two.start()
+    one.wait()
+    two.wait()
 
 
 def per_device(subjects, slabs, template, images, velocity, stiffness, send_rows, ref_slot, columns, weights):
@@ -323,7 +374,7 @@
     cap = send_rows.shape[3]
     slots = slabs * cap
     planes = rows // YR
-    any_space = pl.BlockSpec(memory_space=pl.ANY)
+    hbm_space = pl.BlockSpec(memory_space=pltpu.HBM)
     dma = pltpu.SemaphoreType.DMA
     vm = pltpu.VMEM
     scratch = [
@@ -339,7 +390,7 @@
         vm((NB, rows, width), F32),
         vm((NB, len(OFFSETS), rows, width), F32),
         vm((NB, rows, slots), BF),
-        vm((NB, slots, rows), BF),
+        vm((slots, NB * rows), BF),
         vm((slots, rows), BF),
         vm((rows, slots), BF),
         vm((slots, width), F32),
@@ -347,33 +398,32 @@
         vm((slots, 2 * width), BF),
         vm((rows + 2 * YR, width), F32),
         vm((len(OFFSETS), rows, width), F32),
-        vm((rows, 2 * width), BF),
-        vm((slots, 2 * width), F32),
+        vm((NB * rows, 2 * width), BF),
         vm((slots, width), F32),
-        vm((rows, width), F32),
         vm((rows, width), F32),
         vm((rows, width), F32),
         vm((7, rows + 2 * YR, width), F32),
         vm((rows + 4 * YR, width), F32),
         vm((3, rows + 4 * YR, width), F32),
         vm((3, rows + 2 * YR, width), F32),
-        vm((3, rows, width), F32),
         dma((8,)),
         dma((slabs,)), dma((slabs,)), dma((slabs,)), dma((slabs,)),
         dma((subjects,)), dma((subjects,)), dma((subjects,)), dma((subjects,)),
-        dma((10,)), dma((10,)),
+        dma((subjects,)), dma((subjects,)), dma((10,)), dma((10,)),
     ]
-    return pl.pallas_call(
+    outs = (
+        jax.ShapeDtypeStruct((rows, width), F32),
+        jax.ShapeDtypeStruct((1, 3, rows, width), F32),
+    )
+    vmem_space = pl.BlockSpec(memory_space=vm)
+    new = pl.pallas_call(
         functools.partial(kernel, subjects, slabs, cap),
-        out_shape=(
-            jax.ShapeDtypeStruct((rows, width), F32),
-            jax.ShapeDtypeStruct((1, 3, rows, width), F32),
-        ),
-        in_specs=[any_space] * 8,
-        out_specs=(any_space, any_space),
+        out_shape=tuple(vm(o.shape, o.dtype) for o in outs),
+        in_specs=[hbm_space] * 8,
+        out_specs=(vmem_space, vmem_space),
         scratch_shapes=scratch,
         compiler_params=pltpu.CompilerParams(
-            collective_id=0, has_side_effects=True, vmem_limit_bytes=56 * 2**20
+            collective_id=0, has_side_effects=True, vmem_limit_bytes=62 * 2**20
         ),
     )(
         template, images, velocity, stiffness, send_rows,
@@ -381,6 +431,14 @@
         columns.reshape(rows * NB, width),
         weights.reshape(rows * NB, width),
     )
+    return pl.pallas_call(
+        store,
+        out_shape=outs,
+        in_specs=[pl.BlockSpec(memory_space=pl.ANY)] * 2,
+        out_specs=(hbm_space, hbm_space),
+        scratch_shapes=[dma((2,))],
+        compiler_params=pltpu.CompilerParams(vmem_limit_bytes=2**20),
+    )(*new)
 
 
 def solution(mesh):

time: 52.2 us -> 46.9 us (0.90)
  local copies, waits for them, and re-layouts: 3.73 us -> 0 us
  Pallas kernels: 47.7 us -> 45.9 us
    unnamed x2 -> x0, local copies, waits for them, and re-layouts: 3.73 us -> none
    pallas_call x1, Pallas kernels: 47.7 us -> 44.9 us  [per_device(): pl.pallas_call(functools.partial(kernel, subjects, slabs, cap), out_shape...]
    pallas_call x0 -> x1, Pallas kernels: none -> 0.98 us  [per_device(): pl.pallas_call(store, out_shape=outs, in_specs=[pl.BlockSpec(memory_space...]
where the time goes in v2:
time: 46.9 us; the launch traced here: 46.7 us
  Pallas kernels  45.9 us (98%)
  between operations  0.8 us (2%)
    pallas_call x1, Pallas kernels, per_device(): pl.pallas_call(functools.partial(kernel, subjects, slabs, cap), out_shape...  44.9 us
    pallas_call x1, Pallas kernels, per_device(): pl.pallas_call(store, out_shape=outs, in_specs=[pl.BlockSpec(memory_space...  0.98 us

profile of v2, /device:TPU:1, one launch (start us, length us, event | category | flops | bytes accessed | tf_op | source)
XLA Modules:
  0.0 46.7 jit_solution(9983294531496425664)
XLA Ops:
  0.6 44.9 %shard_map.95 = (f32[512,128]{1,0:T(8,128)S(1)}, f32[1,3,512,128]{3,2,1,0:T(8,128)S(1)}) custom-call(f32[512,128]{1,0:T(8,128)} %tmpl.1, f32[1,512,128]{2,1,0:T(8,128)} %img.1, f32[1,3,512,128]{3,2,1,0:T(8,128)} %vel.1, f32[512,128]{1,0:T(8,128)} %stiff.1, s32[1,1,16,32]{3,2,1,0:T(8,128)} %send.1, s32[1,8,512]{2,1,0:T(8,128)} %bitcast.5, ...), custom_call_target="tpu_custom_call" | custom-call | tf_op jit(solution)/shard_map/pallas_call | solution.py:419
  45.6 1.0 %shard_map.96 = (f32[512,128]{1,0:T(8,128)}, f32[1,3,512,128]{3,2,1,0:T(8,128)}) custom-call(f32[512,128]{1,0:T(8,128)S(1)} %get-tuple-element.4.template, f32[1,3,512,128]{3,2,1,0:T(8,128)S(1)} %get-tuple-element.5.velocity), custom_call_target="tpu_custom_call" | custom-call | tf_op jit(solution)/shard_map/pallas_call | solution.py:434

commit v3 on v2

--- a/solution.py
+++ b/solution.py
@@ -1,4 +1,5 @@
 import functools
+import math
 
 import jax
 import jax.numpy as jnp
@@ -23,8 +24,14 @@
     return hi, lo
 
 
-def far_first(n):
-    return sorted(range(1, n), key=lambda d: -min(d, n - d))
+def torus(outer, inner):
+    hops = lambda d, n: min(d, n - d)
+    every = [(a, b) for a in range(outer) for b in range(inner) if (a, b) != (0, 0)]
+    return sorted(every, key=lambda o: -hops(o[0], outer) - hops(o[1], inner))
+
+
+def shift(me, outer, inner, a, b):
+    return lax.rem(me // inner + a, outer) * inner + lax.rem(lax.rem(me, inner) + b, inner)
 
 
 def kernel(
@@ -46,20 +53,24 @@
         (stiff, stif.at[pl.ds(2 * YR, rows), :]), (img, img_v), (vel, vel_v),
     )
     loads = [pltpu.make_async_copy(a, b, load_sem.at[i]) for i, (a, b) in enumerate(pairs)]
-    for load in loads:
+    for load in loads[:2]:
         load.start()
 
+    side = math.isqrt(subjects)
+    shapes = {"slab": (me_k, slabs // 2, 2), "subj": (me_s, subjects // side, side)}
     barrier = pltpu.get_barrier_semaphore()
-    for d in range(1, slabs):
-        pl.semaphore_signal(barrier, inc=1, device_id={"slab": lax.rem(me_k + d, slabs)})
-    for d in range(1, subjects):
-        pl.semaphore_signal(barrier, inc=1, device_id={"subj": lax.rem(me_s + d, subjects)})
-
-    def peers(axis, n, me, src, dst, send_sem, recv_sem):
+    for z, xy in zip(torus(*shapes["slab"][1:]), torus(*shapes["subj"][1:])):
+        pl.semaphore_signal(barrier, inc=1, device_id={"slab": shift(*shapes["slab"], *z)})
+        pl.semaphore_signal(barrier, inc=1, device_id={"subj": shift(*shapes["subj"], *xy)})
+    for load in loads[2:]:
+        load.start()
+
+    def peers(axis, src, dst, send_sem, recv_sem):
         out = []
-        for d in far_first(n):
-            to = lax.rem(me + d, n)
-            come = lax.rem(me + n - d, n)
+        me, outer, inner = shapes[axis]
+        for a, b in torus(outer, inner):
+            to = shift(me, outer, inner, a, b)
+            come = shift(me, outer, inner, outer - a, inner - b)
             go = pltpu.make_async_remote_copy(
                 src_ref=src(to), dst_ref=dst(me), send_sem=send_sem.at[to], recv_sem=recv_sem.at[me],
                 device_id={axis: to},
@@ -106,7 +117,7 @@
     pl.semaphore_wait(barrier, slabs - 1 + subjects - 1)
     pl.when(linked)(stif_far.start)
     first = peers(
-        "slab", slabs, me_k,
+        "slab",
         lambda j: outbox.at[pl.ds(j * cap, cap), :], lambda k: inbox.at[pl.ds(k * cap, cap), :], a_send, a_recv,
     )
     for go, _ in first:
@@ -139,7 +150,7 @@
             wd[b, n] = pltpu.roll(kept, d % width, 1) if d else kept
 
     shared = peers(
-        "subj", subjects, me_s,
+        "subj",
         lambda s: stif_rows(far_in + me_s * part), lambda s: stif_rows(far_in + s * part), e_send, e_recv,
     )
 
@@ -226,17 +237,19 @@
             hi, lo = halves(total)
             place[pl.ds(b * rows + c * block, block), :width] = hi
             place[pl.ds(b * rows + c * block, block), width:] = lo
-    both = jnp.dot(oht[...], place[...], preferred_element_type=F32)
-
     for go, _ in first:
         go.wait_send()
-    outbox[...] = both[:, :width] + both[:, width:]
     second = peers(
-        "slab", slabs, me_k,
+        "slab",
         lambda j: outbox.at[pl.ds(j * cap, cap), :], lambda k: retbox.at[pl.ds(k * cap, cap), :], b_send, b_recv,
     )
-    for go, _ in second:
-        go.start()
+    for part_of in range(2):
+        here = pl.ds(part_of * (slots // 2), slots // 2)
+        both = jnp.dot(oht[here, :], place[...], preferred_element_type=F32)
+        outbox[here, :] = both[:, :width] + both[:, width:]
+        for (go, _), (a, b) in zip(second, torus(slabs // 2, 2)):
+            to = shift(me_k, slabs // 2, 2, a, b)
+            pl.when(to // (slabs // 2) == part_of)(go.start)
     retbox[own, :] = outbox[own, :]
 
     halo_got(warp_halo)
@@ -298,7 +311,7 @@
     both = jnp.dot(ost[...], jnp.concatenate([hi, lo], axis=1), preferred_element_type=F32)
     rowg[...] = both[:, :width] + both[:, width:]
     third = peers(
-        "subj", subjects, me_s,
+        "subj",
         lambda s: rowg.at[pl.ds(s * part, part), :], lambda s: subbox.at[pl.ds(s * part, part), :], c_send, c_recv,
     )
     for go, _ in third:
@@ -312,7 +325,7 @@
         total = total + subbox[pl.ds(s * part, part), :]
     tout[mine, :] = tmpl_v[mine, :] - (RATE / subjects) * total
     fourth = peers(
-        "subj", subjects, me_s,
+        "subj",
         lambda s: tout.at[mine, :], lambda s: tout.at[pl.ds(pl.multiple_of(s * part, part), part), :], d_send, d_recv,
     )
     for go, _ in fourth:

time: 46.9 us -> 44.6 us (0.951)
  Pallas kernels: 45.9 us -> 43.5 us
    pallas_call x1, Pallas kernels: 44.9 us -> 42.5 us  [per_device(): pl.pallas_call(functools.partial(kernel, subjects, slabs, cap), out_shape...]
where the time goes in v3:
time: 44.6 us; the launch traced here: 44.3 us
  Pallas kernels  43.5 us (98%)
  between operations  0.8 us (2%)
    pallas_call x1, Pallas kernels, per_device(): pl.pallas_call(functools.partial(kernel, subjects, slabs, cap), out_shape...  42.5 us
    pallas_call x1, Pallas kernels, per_device(): pl.pallas_call(store, out_shape=outs, in_specs=[pl.BlockSpec(memory_space...  0.98 us

profile of v3, /device:TPU:1, one launch (start us, length us, event | category | flops | bytes accessed | tf_op | source)
XLA Modules:
  0.0 44.3 jit_solution(12260415235175264111)
XLA Ops:
  0.6 42.5 %shard_map.95 = (f32[512,128]{1,0:T(8,128)S(1)}, f32[1,3,512,128]{3,2,1,0:T(8,128)S(1)}) custom-call(f32[512,128]{1,0:T(8,128)} %tmpl.1, f32[1,512,128]{2,1,0:T(8,128)} %img.1, f32[1,3,512,128]{3,2,1,0:T(8,128)} %vel.1, f32[512,128]{1,0:T(8,128)} %stiff.1, s32[1,1,16,32]{3,2,1,0:T(8,128)} %send.1, s32[1,8,512]{2,1,0:T(8,128)} %bitcast.5, ...), custom_call_target="tpu_custom_call" | custom-call | tf_op jit(solution)/shard_map/pallas_call | solution.py:432
  43.1 1.0 %shard_map.96 = (f32[512,128]{1,0:T(8,128)}, f32[1,3,512,128]{3,2,1,0:T(8,128)}) custom-call(f32[512,128]{1,0:T(8,128)S(1)} %get-tuple-element.4.template, f32[1,3,512,128]{3,2,1,0:T(8,128)S(1)} %get-tuple-element.5.velocity), custom_call_target="tpu_custom_call" | custom-call | tf_op jit(solution)/shard_map/pallas_call | solution.py:447

commit v4 on v3

--- a/solution.py
+++ b/solution.py
@@ -30,15 +30,17 @@
     return sorted(every, key=lambda o: -hops(o[0], outer) - hops(o[1], inner))
 
 
-def shift(me, outer, inner, a, b):
-    return lax.rem(me // inner + a, outer) * inner + lax.rem(lax.rem(me, inner) + b, inner)
+def others(me, outer, inner):
+    a0, b0 = me // inner, lax.rem(me, inner)
+    wrap = lambda at, d, n: jnp.where(at >= n - d, at + d - n, at + d) if d else at
+    return [wrap(a0, a, outer) * inner + wrap(b0, b, inner) for a, b in torus(outer, inner)]
 
 
 def kernel(
     subjects, slabs, cap,
     tmpl, img, vel, stiff, send, slot_t, cols, wts,
     tout, vout,
-    tmpl_v, img_v, vel_v, send_v, slot_v, cols_v, wts_v, w32, colb, wb, wd, oh, oht, os, ost,
+    tmpl_v, img_v, vel_v, send_v, slot_v, cols_v, wts_v, w32, wd, oh, oht, os, ost,
     outbox, inbox, t2, warp, mis, place, retbox, rowg, subbox, coef, stif, field, field1,
     load_sem, a_send, a_recv, b_send, b_recv, c_send, c_recv, d_send, d_recv, e_send, e_recv, h_send, h_recv,
 ):
@@ -57,30 +59,33 @@
         load.start()
 
     side = math.isqrt(subjects)
-    shapes = {"slab": (me_k, slabs // 2, 2), "subj": (me_s, subjects // side, side)}
+    rest = {"slab": others(me_k, slabs // 2, 2), "subj": others(me_s, subjects // side, side)}
     barrier = pltpu.get_barrier_semaphore()
-    for z, xy in zip(torus(*shapes["slab"][1:]), torus(*shapes["subj"][1:])):
-        pl.semaphore_signal(barrier, inc=1, device_id={"slab": shift(*shapes["slab"], *z)})
-        pl.semaphore_signal(barrier, inc=1, device_id={"subj": shift(*shapes["subj"], *xy)})
+    for pair in zip(rest["slab"], rest["subj"]):
+        for axis, to in zip(("slab", "subj"), pair):
+            pl.semaphore_signal(barrier, inc=1, device_id={axis: to})
     for load in loads[2:]:
         load.start()
 
     def peers(axis, src, dst, send_sem, recv_sem):
-        out = []
-        me, outer, inner = shapes[axis]
-        for a, b in torus(outer, inner):
-            to = shift(me, outer, inner, a, b)
-            come = shift(me, outer, inner, outer - a, inner - b)
-            go = pltpu.make_async_remote_copy(
-                src_ref=src(to), dst_ref=dst(me), send_sem=send_sem.at[to], recv_sem=recv_sem.at[me],
-                device_id={axis: to},
+        return [
+            pltpu.make_async_remote_copy(
+                src_ref=src(to), dst_ref=dst(i), send_sem=send_sem.at[i], recv_sem=recv_sem.at[i], device_id={axis: to},
             )
-            got = pltpu.make_async_remote_copy(
-                src_ref=src(to), dst_ref=dst(come), send_sem=send_sem.at[to], recv_sem=recv_sem.at[come],
-                device_id={axis: to},
-            )
-            out.append((go, got))
-        return out
+            for i, to in enumerate(rest[axis])
+        ]
+
+    def start(copies):
+        for copy in copies:
+            copy.start()
+
+    def got(copies):
+        for copy in copies:
+            copy.wait_recv()
+
+    def sent(copies):
+        for copy in copies:
+            copy.wait_send()
 
     loads[0].wait()
     send_c = jnp.transpose(send_v[0, 0])
@@ -116,13 +121,10 @@
 
     pl.semaphore_wait(barrier, slabs - 1 + subjects - 1)
     pl.when(linked)(stif_far.start)
-    first = peers(
-        "slab",
-        lambda j: outbox.at[pl.ds(j * cap, cap), :], lambda k: inbox.at[pl.ds(k * cap, cap), :], a_send, a_recv,
-    )
-    for go, _ in first:
-        go.start()
     own = pl.ds(pl.multiple_of(me_k * cap, cap), cap)
+    to_slab = lambda j: outbox.at[pl.ds(pl.multiple_of(j * cap, cap), cap), :]
+    first = peers("slab", to_slab, lambda i: inbox.at[own, :], a_send, a_recv)
+    start(first)
     inbox[own, :] = outbox[own, :]
 
     stif_near.start()
@@ -130,10 +132,12 @@
     loads[2].wait()
     slot_c = jnp.transpose(slot_v[0])
     lane_q = lax.broadcasted_iota(jnp.int32, (rows, slots), 1)
-    sub_q = lax.broadcasted_iota(jnp.int32, (slots, rows), 0)
+    sub_q = lax.broadcasted_iota(jnp.int32, (slots, width), 0)
     for b in range(NB):
         oh[b] = jnp.where(slot_c[:, b : b + 1] == lane_q, 1.0, 0.0).astype(BF)
-        oht[:, pl.ds(b * rows, rows)] = jnp.where(sub_q == slot_v[0, b : b + 1, :], 1.0, 0.0).astype(BF)
+        for c in range(rows // width):
+            slot = slot_v[0, b : b + 1, c * width : (c + 1) * width]
+            oht[:, pl.ds((c * NB + b) * width, width)] = jnp.where(sub_q == slot, 1.0, 0.0).astype(BF)
     ost[...] = jnp.transpose(os[...].astype(F32)).astype(BF)
     loads[3].wait()
     loads[4].wait()
@@ -142,40 +146,10 @@
     for b in range(NB):
         col = cols_v[pl.ds(b, rows, stride=NB), :]
         wgt = w32[pl.ds(b, rows, stride=NB), :]
-        colb[b] = col
-        wb[b] = wgt
         off = col - lane
         for n, d in enumerate(OFFSETS):
             kept = jnp.where(off == d, wgt, 0.0)
             wd[b, n] = pltpu.roll(kept, d % width, 1) if d else kept
-
-    shared = peers(
-        "subj",
-        lambda s: stif_rows(far_in + me_s * part), lambda s: stif_rows(far_in + s * part), e_send, e_recv,
-    )
-
-    @pl.when(linked)
-    def _():
-        stif_far.wait_recv()
-        for go, _ in shared:
-            go.start()
-
-    for _, got in first:
-        got.wait_recv()
-    hi, lo = halves(inbox[...])
-    t2[:, :width] = hi
-    t2[:, width:] = lo
-    block = rows // 2
-    for c in range(2):
-        here = pl.ds(c * block, block)
-        total = None
-        for b in range(NB):
-            both = jnp.dot(oh[b, here, :], t2[...], preferred_element_type=F32)
-            picked = both[:, :width] + both[:, width:]
-            values = jnp.take_along_axis(picked, colb[b, here, :], axis=1, mode="promise_in_bounds")
-            term = wb[b, here, :] * values
-            total = term if total is None else total + term
-        warp[pl.ds(YR + c * block, block), :] = total
 
     low = lax.rem(me_k + slabs - 1, slabs)
     high = lax.rem(me_k + 1, slabs)
@@ -220,36 +194,65 @@
 
     warp_halo = halo(warp, (), YR, 0)
     field_halo = [halo(field, (a,), 2 * YR, 4 + 2 * a) for a in range(3)]
-    halo_start(warp_halo)
-
+
+    shared = peers(
+        "subj",
+        lambda s: stif_rows(far_in + me_s * part), lambda i: stif_rows(far_in + me_s * part), e_send, e_recv,
+    )
+
+    @pl.when(linked)
+    def _():
+        stif_far.wait_recv()
+        start(shared)
+
+    got(first)
+    hi, lo = halves(inbox[...])
+    t2[:, :width] = hi
+    t2[:, width:] = lo
     loads[6].wait()
-    mis[2] = warp[pl.ds(YR, rows), :] - img_v[0]
-    for n, d in enumerate(OFFSETS):
-        if d:
-            mis[n] = pltpu.roll(mis[2], d % width, 1)
-    block = rows // 8
-    for b in range(NB):
-        for c in range(8):
-            here = pl.ds(c * block, block)
-            total = wd[b, 0, here, :] * mis[0, here, :]
-            for n in range(1, len(OFFSETS)):
-                total = total + wd[b, n, here, :] * mis[n, here, :]
-            hi, lo = halves(total)
-            place[pl.ds(b * rows + c * block, block), :width] = hi
-            place[pl.ds(b * rows + c * block, block), width:] = lo
-    for go, _ in first:
-        go.wait_send()
-    second = peers(
-        "slab",
-        lambda j: outbox.at[pl.ds(j * cap, cap), :], lambda k: retbox.at[pl.ds(k * cap, cap), :], b_send, b_recv,
-    )
+    for c in range(rows // width):
+        here = pl.ds(c * width, width)
+        sums = [None] * len(OFFSETS)
+        for b in range(NB):
+            both = jnp.dot(oh[b, here, :], t2[...], preferred_element_type=F32)
+            picked = both[:, :width] + both[:, width:]
+            for n in range(len(OFFSETS)):
+                term = wd[b, n, here, :] * picked
+                sums[n] = term if sums[n] is None else sums[n] + term
+        total = sums[OFFSETS.index(0)]
+        for n, d in enumerate(OFFSETS):
+            if d:
+                total = total + pltpu.roll(sums[n], -d % width, 1)
+        warp[pl.ds(YR + c * width, width), :] = total
+        apart = total - img_v[0, here, :]
+        for n, d in enumerate(OFFSETS):
+            mis[n, here, :] = pltpu.roll(apart, d % width, 1) if d else apart
+        if (c + 1) * width == YR:
+            pl.when(me_k > 0)(warp_halo[0].start)
+    pl.when(me_k < slabs - 1)(warp_halo[1].start)
+
+    block = 16
+    for c in range(rows // width):
+        for q in range(width // block):
+            here = pl.ds(c * width + q * block, block)
+            apart = [mis[n, here, :] for n in range(len(OFFSETS))]
+            for b in range(NB):
+                total = wd[b, 0, here, :] * apart[0]
+                for n in range(1, len(OFFSETS)):
+                    total = total + wd[b, n, here, :] * apart[n]
+                hi, lo = halves(total)
+                there = pl.ds((c * NB + b) * width + q * block, block)
+                place[there, :width] = hi
+                place[there, width:] = lo
+
+    sent(first)
+    second = peers("slab", to_slab, lambda i: retbox.at[own, :], b_send, b_recv)
     for part_of in range(2):
         here = pl.ds(part_of * (slots // 2), slots // 2)
         both = jnp.dot(oht[here, :], place[...], preferred_element_type=F32)
         outbox[here, :] = both[:, :width] + both[:, width:]
-        for (go, _), (a, b) in zip(second, torus(slabs // 2, 2)):
-            to = shift(me_k, slabs // 2, 2, a, b)
-            pl.when(to // (slabs // 2) == part_of)(go.start)
+        for copy, to in zip(second, rest["slab"]):
+            pl.when((to >= slabs // 2) == bool(part_of))(copy.start)
     retbox[own, :] = outbox[own, :]
 
     halo_got(warp_halo)
@@ -264,27 +267,28 @@
         below = jnp.where(row_p == YR - 1, 0.0, pltpu.roll(x, YR - 1, 0))
         return left, right, above, below
 
-    @pl.loop(0, rows // YR)
-    def _(p):
-        here = pl.ds(pl.multiple_of(p * YR, YR), YR)
-        left, right, above, below = shifted(warp[pl.ds(pl.multiple_of((p + 1) * YR, YR), YR), :])
-        before = warp[here, :]
-        after = warp[pl.ds(pl.multiple_of((p + 2) * YR, YR), YR), :]
-        force = (0.5 * FORCE) * mis[2, here, :]
-        there = pl.ds(pl.multiple_of((p + 2) * YR, YR), YR)
-        field[0, there, :] = vel_v[0, 0, here, :] - force * (right - left)
-        field[1, there, :] = vel_v[0, 1, here, :] - force * (below - above)
-        field[2, there, :] = vel_v[0, 2, here, :] - force * (after - before)
-
-    for h in field_halo:
-        halo_start(h)
+    def along(x, dim):
+        left, right, above, below = shifted(x)
+        return right - left if dim else below - above
+
+    for a in range(3):
+
+        @pl.loop(0, rows // YR)
+        def _(p):
+            plane = lambda i: pl.ds(pl.multiple_of((p + i) * YR, YR), YR)
+            if a == 2:
+                slope = warp[plane(2), :] - warp[plane(0), :]
+            else:
+                slope = along(warp[plane(1), :], 1 - a)
+            field[a, plane(2), :] = vel_v[0, a, plane(0), :] - (0.5 * FORCE) * mis[2, plane(0), :] * slope
+
+        halo_start(field_halo[a])
 
     stif_near.wait_recv()
 
     @pl.when(linked)
     def _():
-        for _, got in shared:
-            got.wait_recv()
+        got(shared)
 
     @pl.loop(0, rows // YR + 2)
     def _(p):
@@ -305,31 +309,25 @@
         coef[5, here, :] = scale * (centre + after)
         coef[6, here, :] = inside - scale * spent
 
-    for _, got in second:
-        got.wait_recv()
+    got(second)
     hi, lo = halves(retbox[...])
-    both = jnp.dot(ost[...], jnp.concatenate([hi, lo], axis=1), preferred_element_type=F32)
-    rowg[...] = both[:, :width] + both[:, width:]
+    back = jnp.concatenate([hi, lo], axis=1)
     third = peers(
-        "subj",
-        lambda s: rowg.at[pl.ds(s * part, part), :], lambda s: subbox.at[pl.ds(s * part, part), :], c_send, c_recv,
-    )
-    for go, _ in third:
-        go.start()
-    subbox[mine, :] = rowg[mine, :]
-
-    for _, got in third:
-        got.wait_recv()
-    total = subbox[pl.ds(0, part), :]
-    for s in range(1, subjects):
-        total = total + subbox[pl.ds(s * part, part), :]
+        "subj", lambda s: rowg.at[pl.ds(pl.multiple_of(s * part, part), part), :], lambda i: subbox.at[i], c_send, c_recv,
+    )
+    for part_of in range(2):
+        here = pl.ds(part_of * (rows // 2), rows // 2)
+        both = jnp.dot(ost[here, :], back, preferred_element_type=F32)
+        rowg[here, :] = both[:, :width] + both[:, width:]
+        for copy, to in zip(third, rest["subj"]):
+            pl.when((to >= subjects // 2) == bool(part_of))(copy.start)
+    total = rowg[mine, :]
+    got(third)
+    for i in range(subjects - 1):
+        total = total + subbox[i]
     tout[mine, :] = tmpl_v[mine, :] - (RATE / subjects) * total
-    fourth = peers(
-        "subj",
-        lambda s: tout.at[mine, :], lambda s: tout.at[pl.ds(pl.multiple_of(s * part, part), part), :], d_send, d_recv,
-    )
-    for go, _ in fourth:
-        go.start()
+    fourth = peers("subj", lambda s: tout.at[mine, :], lambda i: tout.at[mine, :], d_send, d_recv)
+    start(fourth)
 
     def step(src, lead, p, q):
         at = lambda i: pl.ds(pl.multiple_of(i * YR, YR), YR)
@@ -357,11 +355,8 @@
     for a in range(3):
         diffuse(a)
 
-    for _, got in fourth:
-        got.wait_recv()
-    for group in (second, third, fourth):
-        for go, _ in group:
-            go.wait_send()
+    for group in (second, third):
+        sent(group)
     for h in (warp_halo, *field_halo):
         halo_sent(h)
     stif_near.wait_send()
@@ -369,8 +364,10 @@
     @pl.when(linked)
     def _():
         stif_far.wait_send()
-        for go, _ in shared:
-            go.wait_send()
+        sent(shared)
+
+    got(fourth)
+    sent(fourth)
 
 
 def store(template, velocity, tout, vout, sem):
@@ -399,8 +396,6 @@
         vm((rows * NB, width), jnp.int32),
         vm((rows * NB, width), BF),
         vm((rows * NB, width), F32),
-        vm((NB, rows, width), jnp.int32),
-        vm((NB, rows, width), F32),
         vm((NB, len(OFFSETS), rows, width), F32),
         vm((NB, rows, slots), BF),
         vm((slots, NB * rows), BF),
@@ -414,7 +409,7 @@
         vm((NB * rows, 2 * width), BF),
         vm((slots, width), F32),
         vm((rows, width), F32),
-        vm((rows, width), F32),
+        vm((subjects - 1, rows // subjects, width), F32),
         vm((7, rows + 2 * YR, width), F32),
         vm((rows + 4 * YR, width), F32),
         vm((3, rows + 4 * YR, width), F32),

time: 44.6 us -> 44.1 us (0.989)
  Pallas kernels: 43.5 us -> 42.9 us
    pallas_call x1, Pallas kernels: 42.5 us -> 42 us  [per_device(): pl.pallas_call(functools.partial(kernel, subjects, slabs, cap), out_shape...]
where the time goes in v4:
time: 44.1 us; the launch traced here: 43.7 us
  Pallas kernels  42.9 us (97%)
  between operations  0.8 us (2%)
    pallas_call x1, Pallas kernels, per_device(): pl.pallas_call(functools.partial(kernel, subjects, slabs, cap), out_shape...  42 us
    pallas_call x1, Pallas kernels, per_device(): pl.pallas_call(store, out_shape=outs, in_specs=[pl.BlockSpec(memory_space...  0.98 us

profile of v4, /device:TPU:1, one launch (start us, length us, event | category | flops | bytes accessed | tf_op | source)
XLA Modules:
  0.0 43.7 jit_solution(4707639585808499299)
XLA Ops:
  0.6 42.0 %shard_map.95 = (f32[512,128]{1,0:T(8,128)S(1)}, f32[1,3,512,128]{3,2,1,0:T(8,128)S(1)}) custom-call(f32[512,128]{1,0:T(8,128)} %tmpl.1, f32[1,512,128]{2,1,0:T(8,128)} %img.1, f32[1,3,512,128]{3,2,1,0:T(8,128)} %vel.1, f32[512,128]{1,0:T(8,128)} %stiff.1, s32[1,1,16,32]{3,2,1,0:T(8,128)} %send.1, s32[1,8,512]{2,1,0:T(8,128)} %bitcast.5, ...), custom_call_target="tpu_custom_call" | custom-call | tf_op jit(solution)/shard_map/pallas_call | solution.py:427
  42.6 1.0 %shard_map.96 = (f32[512,128]{1,0:T(8,128)}, f32[1,3,512,128]{3,2,1,0:T(8,128)}) custom-call(f32[512,128]{1,0:T(8,128)S(1)} %get-tuple-element.4.template, f32[1,3,512,128]{3,2,1,0:T(8,128)S(1)} %get-tuple-element.5.velocity), custom_call_target="tpu_custom_call" | custom-call | tf_op jit(solution)/shard_map/pallas_call | solution.py:442

commit v5 on v4

--- a/solution.py
+++ b/solution.py
@@ -40,7 +40,7 @@
     subjects, slabs, cap,
     tmpl, img, vel, stiff, send, slot_t, cols, wts,
     tout, vout,
-    tmpl_v, img_v, vel_v, send_v, slot_v, cols_v, wts_v, w32, wd, oh, oht, os, ost,
+    tmpl_v, img_v, vel_v, send_v, slot_v, cols_v, wts_v, w32, wd, oh, oht, os, ost, slot_id, row_id,
     outbox, inbox, t2, warp, mis, place, retbox, rowg, subbox, coef, stif, field, field1,
     load_sem, a_send, a_recv, b_send, b_recv, c_send, c_recv, d_send, d_recv, e_send, e_recv, h_send, h_recv,
 ):
@@ -70,7 +70,7 @@
     def peers(axis, src, dst, send_sem, recv_sem):
         return [
             pltpu.make_async_remote_copy(
-                src_ref=src(to), dst_ref=dst(i), send_sem=send_sem.at[i], recv_sem=recv_sem.at[i], device_id={axis: to},
+                src_ref=src(i, to), dst_ref=dst(i), send_sem=send_sem.at[i], recv_sem=recv_sem.at[i], device_id={axis: to},
             )
             for i, to in enumerate(rest[axis])
         ]
@@ -117,28 +117,33 @@
         src_ref=stif_rows(own_at + me_s * part), dst_ref=stif_rows(far_out + me_s * part),
         send_sem=h_send.at[3], recv_sem=h_recv.at[3], device_id={"slab": jnp.clip(across, 0, slabs - 1)},
     )
-    loads[5].wait()
-
     pl.semaphore_wait(barrier, slabs - 1 + subjects - 1)
-    pl.when(linked)(stif_far.start)
     own = pl.ds(pl.multiple_of(me_k * cap, cap), cap)
-    to_slab = lambda j: outbox.at[pl.ds(pl.multiple_of(j * cap, cap), cap), :]
+    to_slab = lambda i, j: outbox.at[pl.ds(pl.multiple_of(j * cap, cap), cap), :]
     first = peers("slab", to_slab, lambda i: inbox.at[own, :], a_send, a_recv)
     start(first)
     inbox[own, :] = outbox[own, :]
 
+    loads[5].wait()
+    pl.when(linked)(stif_far.start)
     stif_near.start()
 
     loads[2].wait()
     slot_c = jnp.transpose(slot_v[0])
     lane_q = lax.broadcasted_iota(jnp.int32, (rows, slots), 1)
-    sub_q = lax.broadcasted_iota(jnp.int32, (slots, width), 0)
+    for i, to in enumerate([*rest["slab"], me_k]):
+        slot_id[pl.ds(i * cap, cap), :] = lax.broadcasted_iota(jnp.int32, (cap, width), 0) + to * cap
+    for i, to in enumerate([*rest["subj"], me_s]):
+        row_id[pl.ds(i * part, part), :] = lax.broadcasted_iota(jnp.int32, (part, width), 0) + to * part
     for b in range(NB):
         oh[b] = jnp.where(slot_c[:, b : b + 1] == lane_q, 1.0, 0.0).astype(BF)
         for c in range(rows // width):
             slot = slot_v[0, b : b + 1, c * width : (c + 1) * width]
-            oht[:, pl.ds((c * NB + b) * width, width)] = jnp.where(sub_q == slot, 1.0, 0.0).astype(BF)
-    ost[...] = jnp.transpose(os[...].astype(F32)).astype(BF)
+            oht[:, pl.ds((c * NB + b) * width, width)] = jnp.where(slot_id[...] == slot, 1.0, 0.0).astype(BF)
+    for t in range(slots // width):
+        held = [jnp.broadcast_to(send_c[:, j : j + 1], (cap, width)) for j in range(t * width // cap, (t + 1) * width // cap)]
+        row = jnp.transpose(jnp.concatenate(held, axis=0))[:1, :]
+        ost[:, pl.ds(t * width, width)] = jnp.where(row_id[...] == row, 1.0, 0.0).astype(BF)
     loads[3].wait()
     loads[4].wait()
     w32[...] = wts_v[...].astype(F32)
@@ -197,7 +202,7 @@
 
     shared = peers(
         "subj",
-        lambda s: stif_rows(far_in + me_s * part), lambda i: stif_rows(far_in + me_s * part), e_send, e_recv,
+        lambda i, s: stif_rows(far_in + me_s * part), lambda i: stif_rows(far_in + me_s * part), e_send, e_recv,
     )
 
     @pl.when(linked)
@@ -246,14 +251,13 @@
                 place[there, width:] = lo
 
     sent(first)
-    second = peers("slab", to_slab, lambda i: retbox.at[own, :], b_send, b_recv)
+    second = peers("slab", lambda i, j: outbox.at[pl.ds(i * cap, cap), :], lambda i: retbox.at[own, :], b_send, b_recv)
     for part_of in range(2):
         here = pl.ds(part_of * (slots // 2), slots // 2)
         both = jnp.dot(oht[here, :], place[...], preferred_element_type=F32)
         outbox[here, :] = both[:, :width] + both[:, width:]
-        for copy, to in zip(second, rest["slab"]):
-            pl.when((to >= slabs // 2) == bool(part_of))(copy.start)
-    retbox[own, :] = outbox[own, :]
+        start(second[part_of * slabs // 2 : (part_of + 1) * slabs // 2])
+    retbox[own, :] = outbox[pl.ds(slots - cap, cap), :]
 
     halo_got(warp_halo)
     loads[7].wait()
@@ -313,20 +317,19 @@
     hi, lo = halves(retbox[...])
     back = jnp.concatenate([hi, lo], axis=1)
     third = peers(
-        "subj", lambda s: rowg.at[pl.ds(pl.multiple_of(s * part, part), part), :], lambda i: subbox.at[i], c_send, c_recv,
+        "subj", lambda i, s: rowg.at[pl.ds(i * part, part), :], lambda i: subbox.at[i], c_send, c_recv,
     )
     for part_of in range(2):
         here = pl.ds(part_of * (rows // 2), rows // 2)
         both = jnp.dot(ost[here, :], back, preferred_element_type=F32)
         rowg[here, :] = both[:, :width] + both[:, width:]
-        for copy, to in zip(third, rest["subj"]):
-            pl.when((to >= subjects // 2) == bool(part_of))(copy.start)
-    total = rowg[mine, :]
+        start(third[part_of * subjects // 2 : (part_of + 1) * subjects // 2])
+    total = rowg[pl.ds(rows - part, part), :]
     got(third)
     for i in range(subjects - 1):
         total = total + subbox[i]
     tout[mine, :] = tmpl_v[mine, :] - (RATE / subjects) * total
-    fourth = peers("subj", lambda s: tout.at[mine, :], lambda i: tout.at[mine, :], d_send, d_recv)
+    fourth = peers("subj", lambda i, s: tout.at[mine, :], lambda i: tout.at[mine, :], d_send, d_recv)
     start(fourth)
 
     def step(src, lead, p, q):
@@ -401,6 +404,8 @@
         vm((slots, NB * rows), BF),
         vm((slots, rows), BF),
         vm((rows, slots), BF),
+        vm((slots, width), jnp.int32),
+        vm((rows, width), jnp.int32),
         vm((slots, width), F32),
         vm((slots, width), F32),
         vm((slots, 2 * width), BF),

time: 44.1 us -> 44.1 us (level)
  no operation moved by 1% of the time
where the time goes in v5:
time: 44.1 us; the launch traced here: 43.3 us
  Pallas kernels  42.5 us (96%)
  between operations  0.8 us (2%)
    pallas_call x1, Pallas kernels, per_device(): pl.pallas_call(functools.partial(kernel, subjects, slabs, cap), out_shape...  41.5 us
    pallas_call x1, Pallas kernels, per_device(): pl.pallas_call(store, out_shape=outs, in_specs=[pl.BlockSpec(memory_space...  0.98 us

profile of v5, /device:TPU:1, one launch (start us, length us, event | category | flops | bytes accessed | tf_op | source)
XLA Modules:
  0.0 43.3 jit_solution(17188430507631434091)
XLA Ops:
  0.6 41.5 %shard_map.95 = (f32[512,128]{1,0:T(8,128)S(1)}, f32[1,3,512,128]{3,2,1,0:T(8,128)S(1)}) custom-call(f32[512,128]{1,0:T(8,128)} %tmpl.1, f32[1,512,128]{2,1,0:T(8,128)} %img.1, f32[1,3,512,128]{3,2,1,0:T(8,128)} %vel.1, f32[512,128]{1,0:T(8,128)} %stiff.1, s32[1,1,16,32]{3,2,1,0:T(8,128)} %send.1, s32[1,8,512]{2,1,0:T(8,128)} %bitcast.5, ...), custom_call_target="tpu_custom_call" | custom-call | tf_op jit(solution)/shard_map/pallas_call | solution.py:432
  42.2 1.0 %shard_map.96 = (f32[512,128]{1,0:T(8,128)}, f32[1,3,512,128]{3,2,1,0:T(8,128)}) custom-call(f32[512,128]{1,0:T(8,128)S(1)} %get-tuple-element.4.template, f32[1,3,512,128]{3,2,1,0:T(8,128)S(1)} %get-tuple-element.5.velocity), custom_call_target="tpu_custom_call" | custom-call | tf_op jit(solution)/shard_map/pallas_call | solution.py:447

commit v6 on v4

--- a/solution.py
+++ b/solution.py
@@ -138,7 +138,6 @@
         for c in range(rows // width):
             slot = slot_v[0, b : b + 1, c * width : (c + 1) * width]
             oht[:, pl.ds((c * NB + b) * width, width)] = jnp.where(sub_q == slot, 1.0, 0.0).astype(BF)
-    ost[...] = jnp.transpose(os[...].astype(F32)).astype(BF)
     loads[3].wait()
     loads[4].wait()
     w32[...] = wts_v[...].astype(F32)
@@ -199,11 +198,6 @@
         "subj",
         lambda s: stif_rows(far_in + me_s * part), lambda i: stif_rows(far_in + me_s * part), e_send, e_recv,
     )
-
-    @pl.when(linked)
-    def _():
-        stif_far.wait_recv()
-        start(shared)
 
     got(first)
     hi, lo = halves(inbox[...])
@@ -254,6 +248,13 @@
         for copy, to in zip(second, rest["slab"]):
             pl.when((to >= slabs // 2) == bool(part_of))(copy.start)
     retbox[own, :] = outbox[own, :]
+
+    @pl.when(linked)
+    def _():
+        stif_far.wait_recv()
+        start(shared)
+
+    ost[...] = jnp.transpose(os[...].astype(F32)).astype(BF)
 
     halo_got(warp_halo)
     loads[7].wait()

time: 44.1 us -> 44 us (level)
  no operation moved by 1% of the time
where the time goes in v6:
time: 44 us; the launch traced here: 43.6 us
  Pallas kernels  43 us (98%)
  between operations  0.64 us (1%)
    pallas_call x1, Pallas kernels, per_device(): pl.pallas_call(functools.partial(kernel, subjects, slabs, cap), out_shape...  42 us
    pallas_call x1, Pallas kernels, per_device(): pl.pallas_call(store, out_shape=outs, in_specs=[pl.BlockSpec(memory_space...  0.98 us

profile of v6, /device:TPU:1, one launch (start us, length us, event | category | flops | bytes accessed | tf_op | source)
XLA Modules:
  0.0 43.6 jit_solution(14580124771371005583)
XLA Ops:
  0.6 42.0 %shard_map.95 = (f32[512,128]{1,0:T(8,128)S(1)}, f32[1,3,512,128]{3,2,1,0:T(8,128)S(1)}) custom-call(f32[512,128]{1,0:T(8,128)} %tmpl.1, f32[1,512,128]{2,1,0:T(8,128)} %img.1, f32[1,3,512,128]{3,2,1,0:T(8,128)} %vel.1, f32[512,128]{1,0:T(8,128)} %stiff.1, s32[1,1,16,32]{3,2,1,0:T(8,128)} %send.1, s32[1,8,512]{2,1,0:T(8,128)} %bitcast.5, ...), custom_call_target="tpu_custom_call" | custom-call | tf_op jit(solution)/shard_map/pallas_call | solution.py:428
  42.6 1.0 %shard_map.96 = (f32[512,128]{1,0:T(8,128)}, f32[1,3,512,128]{3,2,1,0:T(8,128)}) custom-call(f32[512,128]{1,0:T(8,128)S(1)} %get-tuple-element.4.template, f32[1,3,512,128]{3,2,1,0:T(8,128)S(1)} %get-tuple-element.5.velocity), custom_call_target="tpu_custom_call" | custom-call | tf_op jit(solution)/shard_map/pallas_call | solution.py:443
